TPU v7x, 128 devices: a whole 4x4x4 slice. The times are simulated.
128 devices in a mesh: dp: 32 (over z, x, core), pool: 4 (over y).
Axes of the slice: x: 4, y: 4, z: 4, core: 2. Of those that a mesh axis runs over, the one named last changes fastest.
Arguments:
- queries: float32 [1024, 4096], P(('dp', 'pool')), may hold values from -1 to 1, as said below
- documents: float32 [1024, 4096], P(('dp', 'pool')), may hold values from -1 to 1
- document_pool: float32 [65536, 4096], P(('dp', 'pool')), may hold values from -1 to 1
- hard_negatives: int32 [1024, 16], P(('dp', 'pool')), may hold values from 0 to 65535, as said below
Outputs:
- averaged_objective: float32 [], replicated
- query_grad: float32 [1024, 4096], P(('dp', 'pool'))
- document_grad: float32 [1024, 4096], P(('dp', 'pool'))
- pool_grad: float32 [65536, 4096], P(('dp', 'pool'))
Inputs may be any that keep to these rules, and one draw needn't show every extreme that they name: `queries`: rows are noisy embeddings of several scales; entries lie in the stated range. `hard_negatives`: of the 128 ids held by one device, at most 2 lie in the rows k * 512 to (k + 1) * 512 - 1 for any k, and exactly 2 do so for at least 16 values of k; some ids repeat.
All inputs are finite; a program needn't handle non-finite values.
Results may differ from a plain program's by a relative error of at most 0.0003.
Values sent between devices are 32-bit elements; how exact they have to be, the bound alone decides.
No kernel may reach another device: no remote copies, remote signals or barrier semaphores. Data moves between devices by JAX's collectives and lax.ppermute only.
A program may use at most 128 MiB of HBM per device.

v0:
```python
import functools

import jax
import jax.numpy as jnp
from jax import lax
from jax.experimental import pallas as pl
from jax.experimental.pallas import tpu as pltpu
from jax.sharding import PartitionSpec as P

heat = 20.0
epsilon = 1e-06
highest = lax.Precision.HIGHEST
lanes = 128
everyone = ("dp", "pool")
capacity = 2
limit = 56 * 1024 * 1024


def halves(values):
    high = values.astype(jnp.bfloat16)
    return high, (values - high.astype(jnp.float32)).astype(jnp.bfloat16)


def dot3(left, right, contract):
    one = lambda a, b: lax.dot_general(
        a, b, (contract, ((), ())), preferred_element_type=jnp.float32
    )
    return one(left[0], right[0]) + (one(left[0], right[1]) + one(left[1], right[0]))


def pick_kernel(own, asked, pool, *refs):
    packed, done, held, landed, sent = refs[-5:]
    pieces = sent.shape[0]
    part = held.shape[0] // pieces

    def fetch(code, tile, slot):
        row = lax.div(code, own)
        return pltpu.make_async_copy(
            pool.at[lax.div(row, 8), :, lax.rem(row, 8)], held.at[tile, slot], landed
        )

    def start(tile, count):
        for slot in range(8):
            code = asked[tile * (8 // capacity) + slot // capacity, slot % capacity]

            @pl.when(code >= 0)
            def _(code=code, slot=slot):
                fetch(code, tile, slot).start()

            count = count + (code >= 0).astype(jnp.int32)
        return count

    def wait(j, carry):
        fetch(0, 0, 0).wait()
        return carry

    def send(i):
        rows = pl.ds(i * part, part)
        return pltpu.make_async_copy(held.at[rows], packed.at[rows], sent.at[i])

    lax.fori_loop(0, lax.fori_loop(0, held.shape[0], start, 0), wait, 0)
    for i in range(pieces):
        send(i).start()
    done[...] = jnp.zeros_like(done)
    for i in range(pieces):
        send(i).wait()


def pick(asked, own, pool, *earlier):
    total = asked.shape[0] * capacity
    pool_rows, width = pool.shape
    pool = pool.reshape(pool_rows // 8, 8, width // lanes, lanes).transpose(0, 2, 1, 3)
    anywhere = pl.BlockSpec(memory_space=pl.ANY)
    shape = (total // 8, 8, width // lanes, lanes)
    return pl.pallas_call(
        functools.partial(pick_kernel, own),
        in_specs=[pl.BlockSpec(memory_space=pltpu.SMEM), anywhere] + [anywhere] * len(earlier),
        out_specs=[anywhere, pl.BlockSpec(memory_space=pltpu.VMEM)],
        scratch_shapes=[
            pltpu.VMEM(shape, jnp.float32),
            pltpu.SemaphoreType.DMA,
            pltpu.SemaphoreType.DMA((4,)),
        ],
        out_shape=[jax.ShapeDtypeStruct(shape, jnp.float32), jax.ShapeDtypeStruct((8, lanes), jnp.float32)],
        compiler_params=pltpu.CompilerParams(vmem_limit_bytes=limit),
        cost_estimate=pl.CostEstimate(flops=0, bytes_accessed=8 * width * total, transcendentals=0),
    )(asked, pool, *earlier)


def clear_kernel(blank, zeros, fill_sem):
    rows = zeros.shape[0]
    zeros[...] = jnp.zeros_like(zeros)
    fills = [
        pltpu.make_async_copy(zeros, blank.at[pl.ds(i * rows, rows)], fill_sem.at[i])
        for i in range(blank.shape[0] // rows)
    ]
    for fill in fills:
        fill.start()
    for fill in fills:
        fill.wait()


def clear(rows, width, earlier):
    step = 64
    return pl.pallas_call(
        lambda _, *refs: clear_kernel(*refs),
        in_specs=[pl.BlockSpec(memory_space=pl.ANY)],
        out_specs=pl.BlockSpec(memory_space=pl.ANY),
        out_shape=jax.ShapeDtypeStruct((rows, width), jnp.float32),
        scratch_shapes=[pltpu.VMEM((step, width), jnp.float32), pltpu.SemaphoreType.DMA((rows // step,))],
        cost_estimate=pl.CostEstimate(flops=0, bytes_accessed=4 * rows * width, transcendentals=0),
    )(earlier)


def row_fetches(packed, tiles, came, i, step):
    part = pl.ds(i * step, step)
    return [pltpu.make_async_copy(packed.at[:, s, part], tiles.at[:, part, s], came.at[i, s]) for s in range(8)]


def against_kernel(packed, unit, asker, named, *refs):
    parts, scaled, tiles, came = refs[-4:]
    own, count = parts.shape
    strips = tiles.shape[1]
    step = 8
    for i in range(strips // step):
        for fetch in row_fetches(packed, tiles, came, i, step):
            fetch.start()
    real = named[...] >= 0
    scores = jnp.zeros((own, count), jnp.float32)
    squares = jnp.zeros((count, lanes), jnp.float32)
    for i in range(strips // step):
        for fetch in row_fetches(packed, tiles, came, i, step):
            fetch.wait()
        pieces = []
        for j in range(step):
            piece = jnp.where(real, tiles[:, i * step + j].reshape(count, lanes), 0.0)
            squares = squares + piece * piece
            pieces.append(piece)
        columns = slice(i * step * lanes, (i + 1) * step * lanes)
        block = halves(jnp.concatenate(pieces, axis=1))
        scores = scores + dot3(halves(unit[:, columns]), block, ((1,), (1,)))
    scale = lax.rsqrt(jnp.sum(squares, axis=1, keepdims=True) + epsilon)
    scale = jnp.transpose(jnp.broadcast_to(scale, squares.shape))[:own]
    number = lax.broadcasted_iota(jnp.int32, scores.shape, 0)
    chosen = jnp.where(asker[...] == number, jnp.exp(heat * scale * scores - heat), 0.0)
    parts[...] = chosen
    scaled[...] = chosen * scale


def against(packed, unit, asker, *earlier):
    own, width = unit.shape
    groups = packed.shape[0]
    vmem = pl.BlockSpec(memory_space=pltpu.VMEM)
    anywhere = pl.BlockSpec(memory_space=pl.ANY)
    return pl.pallas_call(
        against_kernel,
        in_specs=[anywhere, vmem, vmem, vmem] + [anywhere] * len(earlier),
        out_specs=[vmem, vmem],
        out_shape=[jax.ShapeDtypeStruct((own, 8 * groups), jnp.float32)] * 2,
        scratch_shapes=[
            pltpu.VMEM((groups, width // lanes, 8, lanes), jnp.float32),
            pltpu.SemaphoreType.DMA((width // lanes // 8, 8)),
        ],
        compiler_params=pltpu.CompilerParams(vmem_limit_bytes=limit),
        cost_estimate=pl.CostEstimate(
            flops=48 * own * groups * width, bytes_accessed=32 * width * groups, transcendentals=0
        ),
    )(packed, unit, asker[None, :], jnp.broadcast_to(asker[:, None], (8 * groups, lanes)), *earlier)


def mix_kernel(packed, scaled, named, mixed, tiles, came):
    own, count = scaled.shape
    strips = tiles.shape[1]
    step = 8
    for i in range(strips // step):
        for fetch in row_fetches(packed, tiles, came, i, step):
            fetch.start()
    real = named[...] >= 0
    left = halves(scaled[...])
    for i in range(strips // step):
        for fetch in row_fetches(packed, tiles, came, i, step):
            fetch.wait()
        pieces = [
            jnp.where(real, tiles[:, i * step + j].reshape(count, lanes), 0.0) for j in range(step)
        ]
        columns = slice(i * step * lanes, (i + 1) * step * lanes)
        mixed[:, columns] = dot3(left, halves(jnp.concatenate(pieces, axis=1)), ((1,), (0,)))


def mix(packed, scaled, asker):
    own, count = scaled.shape
    groups, _, strips, _ = packed.shape
    vmem = pl.BlockSpec(memory_space=pltpu.VMEM)
    return pl.pallas_call(
        mix_kernel,
        in_specs=[pl.BlockSpec(memory_space=pl.ANY), vmem, vmem],
        out_specs=vmem,
        out_shape=jax.ShapeDtypeStruct((own, strips * lanes), jnp.float32),
        scratch_shapes=[
            pltpu.VMEM((groups, strips, 8, lanes), jnp.float32),
            pltpu.SemaphoreType.DMA((strips // 8, 8)),
        ],
        compiler_params=pltpu.CompilerParams(vmem_limit_bytes=limit),
        cost_estimate=pl.CostEstimate(
            flops=6 * own * count * strips * lanes, bytes_accessed=4 * count * strips * lanes, transcendentals=0
        ),
    )(packed, scaled, jnp.broadcast_to(asker[:, None], (count, lanes)))


def finish_kernel(
    count, slot_of, row_of, weight, queries, packed, doc_unit, doc_factor, blank,
    doc_grad, pool_grad, held, tiles, upstream, inner, squares, high, low, query_sem, came, row_sem,
):
    slots = inner.shape[0]
    width = queries.shape[1]
    own = doc_unit.shape[0]
    step = 4
    block = step * lanes

    def query_copy(i):
        columns = pl.ds(i * block, block)
        return pltpu.make_async_copy(queries.at[:, columns], held.at[:, columns], query_sem.at[i])

    for i in range(width // block):
        query_copy(i).start()
        for fetch in row_fetches(packed, tiles, came, i, step):
            fetch.start()
    first, second = halves(weight[...])
    high[...] = first
    low[...] = second
    inner[...] = jnp.zeros_like(inner)
    squares[...] = jnp.zeros_like(squares)
    for i in range(width // block):
        columns = slice(i * block, (i + 1) * block)
        query_copy(i).wait()
        above = dot3((high[...], low[...]), halves(held[:, columns]), ((1,), (0,)))
        upstream[:, columns] = above
        for fetch in row_fetches(packed, tiles, came, i, step):
            fetch.wait()
        along, square = inner[...], squares[...]
        for j in range(step):
            piece = tiles[:, i * step + j].reshape(slots, lanes)
            along = along + above[:slots, j * lanes : (j + 1) * lanes] * piece
            square = square + piece * piece
        inner[...] = along
        squares[...] = square

    above = upstream[pl.ds(slots, own), :]
    along = jnp.sum(doc_unit[...] * above, axis=1, keepdims=True)
    doc_grad[...] = doc_factor[:, :1] * (above - doc_unit[...] * along)

    factor = lax.rsqrt(jnp.sum(squares[...], axis=1, keepdims=True) + epsilon)
    along = jnp.sum(inner[...], axis=1, keepdims=True) * factor * factor * factor
    squares[...] = jnp.broadcast_to(factor, squares.shape)
    inner[...] = jnp.broadcast_to(along, inner.shape)

    def row_copy(j):
        return pltpu.make_async_copy(
            upstream.at[pl.ds(slot_of[j], 1)], pool_grad.at[pl.ds(row_of[j], 1)], row_sem
        )

    group = 32

    def settle(tile, sent):
        for i in range(group // 8):
            rows = pl.ds(pl.multiple_of(tile * group + i * 8, 8), 8)
            factor, along = squares[rows, :], inner[rows, :]
            for strip in range(width // lanes):
                columns = slice(strip * lanes, (strip + 1) * lanes)
                upstream[rows, columns] = (
                    factor * upstream[rows, columns] - along * tiles[tile * (group // 8) + i, strip]
                )

        def send(j):
            row_copy(j).start()
            return j + 1

        return lax.while_loop(
            lambda j: (j < count[0]) & (slot_of[jnp.minimum(j, slots - 1)] < (tile + 1) * group), send, sent
        )

    lax.fori_loop(0, slots // group, settle, 0)

    def drain(j, carry):
        row_copy(j).wait()
        return carry

    lax.fori_loop(0, count[0], drain, 0)


def finish(count, slot_of, row_of, weight, queries, packed, doc_unit, doc_factor, blank):
    groups, _, strips, _ = packed.shape
    slots = 8 * groups
    own, width = doc_unit.shape
    batch = queries.shape[0]
    steps = strips // 4
    total = slots + 2 * own
    weight = jnp.pad(weight, ((0, total - weight.shape[0]), (0, 0)))
    vmem = pl.BlockSpec(memory_space=pltpu.VMEM)
    anywhere = pl.BlockSpec(memory_space=pl.ANY)
    smem = pl.BlockSpec(memory_space=pltpu.SMEM)
    return pl.pallas_call(
        finish_kernel,
        in_specs=[smem, smem, smem, vmem, anywhere, anywhere, vmem, vmem, anywhere],
        out_specs=[vmem, anywhere],
        scratch_shapes=[
            pltpu.VMEM((batch, width), jnp.float32),
            pltpu.VMEM((groups, strips, 8, lanes), jnp.float32),
            pltpu.VMEM((total, width), jnp.float32),
            pltpu.VMEM((slots, lanes), jnp.float32),
            pltpu.VMEM((slots, lanes), jnp.float32),
            pltpu.VMEM((total, batch), jnp.bfloat16),
            pltpu.VMEM((total, batch), jnp.bfloat16),
            pltpu.SemaphoreType.DMA((steps,)),
            pltpu.SemaphoreType.DMA((steps, 8)),
            pltpu.SemaphoreType.DMA,
        ],
        out_shape=[
            jax.ShapeDtypeStruct((own, width), jnp.float32),
            jax.ShapeDtypeStruct(blank.shape, jnp.float32),
        ],
        input_output_aliases={8: 1},
        compiler_params=pltpu.CompilerParams(vmem_limit_bytes=limit),
        cost_estimate=pl.CostEstimate(
            flops=6 * total * batch * width, bytes_accessed=4 * width * (batch + 2 * slots), transcendentals=0
        ),
    )(count, slot_of, row_of, weight, queries, packed, doc_unit, doc_factor, blank)


def factor_of(values):
    return lax.rsqrt(jnp.sum(values * values, axis=-1, keepdims=True) + epsilon)


def dot(left, right, contract):
    return lax.dot_general(
        left, right, (contract, ((), ())), precision=highest, preferred_element_type=jnp.float32
    )


def back(factor, unit, upstream):
    return factor * (upstream - unit * jnp.sum(unit * upstream, axis=-1, keepdims=True))


def forward(values, steps):
    return lax.ppermute(values, "pool", [(i, (i + steps) % 4) for i in range(4)])


def ahead(values, direction, size):
    z, x, core = direction
    number = lambda i, j, k: i % 4 * 8 + j % 4 * 2 + k % 2
    blocks = [values]
    for n in range(1, size):
        pairs = [
            (number(i + n * z, j + n * x, k + n * core), number(i, j, k))
            for i in range(4)
            for j in range(4)
            for k in range(2)
        ]
        blocks.append(lax.ppermute(values, "dp", pairs))
    return jnp.concatenate(blocks, axis=0)


def local(queries, documents, document_pool, hard_negatives):
    own, width = queries.shape
    strips = width // lanes
    pool_rows = document_pool.shape[0]
    neg = hard_negatives.shape[1]
    groups = lax.axis_size("dp")
    pool_size = lax.axis_size("pool")
    devices = groups * pool_size
    batch = own * devices
    slots = devices * capacity
    ids = own * neg
    member = lax.axis_index("pool")
    me = lax.axis_index("dp") * pool_size + member

    def exchange(values):
        return lax.all_to_all(values, everyone, split_axis=0, concat_axis=0, tiled=True)

    flat = hard_negatives.reshape(-1)
    owner = flat // pool_rows
    order = jnp.arange(ids, dtype=jnp.int32)
    earlier = (owner[:, None] == owner[None, :]) & (order[None, :] < order[:, None])
    slot = owner * capacity + jnp.sum(earlier.astype(jnp.int32), axis=1)
    asker = order // neg
    taken = slot[None, :] == jnp.arange(slots, dtype=jnp.int32)[:, None]
    code = (flat - owner * pool_rows) * own + asker
    request = jnp.sum(jnp.where(taken, code[None, :] + 1, 0), axis=1) - 1
    slot_query = jnp.sum(jnp.where(taken, asker[None, :] + 1, 0), axis=1) - 1
    request = request.reshape(devices, capacity)
    request = jnp.pad(request, ((0, 0), (0, lanes - capacity)), constant_values=-1)
    asked = exchange(request)

    doc_factor = factor_of(documents)
    doc_unit = documents * doc_factor
    query_factor = factor_of(queries)
    query_unit = queries * query_factor
    everything = lax.all_gather(query_unit, everyone, axis=0, tiled=True)
    passages = ahead(doc_unit, (1, 0, 0), 4)

    cohort = jnp.where(passages[-1, 0] >= -2.0, query_unit, 0.0)
    cohort = jnp.concatenate(
        [cohort] + [forward(cohort, -steps) for steps in range(1, pool_size)], axis=0
    )
    packed, done = pick(asked, own, document_pool, passages, cohort)
    neg_rows = exchange(packed.reshape(devices, capacity * strips, lanes)).reshape(packed.shape)

    picked = done[0, 0] >= 0.0
    arrived = jnp.where(picked, asked[:, :capacity].reshape(-1), -1)
    valid = arrived >= 0
    named_row = jnp.maximum(arrived, 0) // own
    place = jnp.arange(slots, dtype=jnp.int32) // capacity * own + jnp.maximum(arrived, 0) % own
    blank = clear(pool_rows, width, done)

    passages = ahead(ahead(passages, (0, 1, 0), 4), (0, 0, 1), 2)
    parts = jnp.exp(heat * dot(cohort, passages, ((1,), (1,))) - heat)
    sums = jnp.sum(parts, axis=1)

    neg_parts, neg_scaled = against(neg_rows, query_unit, slot_query, sums, blank)

    diagonal = heat * jnp.sum(query_unit * doc_unit, axis=1)
    block = jnp.roll(parts.reshape(pool_size, own, groups * own), member, axis=0)
    block = block.reshape(own * pool_size, groups * own).T.reshape(2, 4, 4, own, own * pool_size)
    block = block.transpose(2, 1, 0, 3, 4)
    for axis, index in enumerate((me // 32, me // 8 % 4, me // 4 % 2)):
        block = jnp.roll(block, index, axis=axis)
    block = block.reshape(groups, 1, -1)
    here = jnp.arange(pool_size, dtype=jnp.int32)[None, :, None] == member
    sums = jnp.roll(sums.reshape(pool_size, own), member, axis=0).reshape(-1)
    news = jnp.concatenate(
        [
            jnp.where(here, block, 0.0).reshape(devices, -1),
            jnp.broadcast_to(sums, (devices, own * pool_size)),
            jnp.broadcast_to(jnp.sum(neg_parts, axis=1), (devices, own)),
            jnp.broadcast_to(diagonal, (devices, own)),
            jnp.sum(neg_parts, axis=0).reshape(devices, capacity),
        ],
        axis=1,
    )
    news = exchange(news)
    edge = own * own * pool_size
    shared = edge + own * pool_size
    both = jnp.sum(news[:, :shared].reshape(groups, pool_size, shared), axis=1)
    doc_parts = both[:, :edge].reshape(groups, own, own * pool_size).transpose(1, 0, 2)
    all_totals = both[:, edge:].reshape(devices, own) + news[:, shared : shared + own]
    all_diagonal = news[:, shared + own : shared + 2 * own]
    slot_parts = news[:, shared + 2 * own :].reshape(-1)
    objective = jnp.sum(jnp.log(all_totals) + heat - all_diagonal) / batch

    scale = heat / all_totals.reshape(1, batch)
    number = jnp.arange(batch, dtype=jnp.int32)[None, :]
    matched = number == me * own + jnp.arange(own, dtype=jnp.int32)[:, None]
    doc_weight = doc_parts.reshape(own, batch) * scale - heat * matched.astype(jnp.float32)
    slot_order = jnp.arange(slots, dtype=jnp.int32)
    spread = jnp.where(place[:, None] == number, slot_parts[:, None], 0.0)
    same = (named_row[:, None] == named_row[None, :]) & valid[None, :]
    spread = dot(same.astype(jnp.float32), spread, ((1,), (0,))) * scale
    repeated = jnp.any(same & (slot_order[None, :] < slot_order[:, None]), axis=1)
    written = valid & ~repeated
    rank = jnp.cumsum(written.astype(jnp.int32)) - 1
    listed = (rank[None, :] == slot_order[:, None]) & written[None, :]
    slot_of = jnp.sum(jnp.where(listed, slot_order[None, :], 0), axis=1)
    row_of = jnp.sum(jnp.where(listed, named_row[None, :], 0), axis=1)
    document_grad, pool_grad = finish(
        jnp.sum(written.astype(jnp.int32))[None],
        slot_of,
        row_of,
        jnp.concatenate([spread, doc_weight], axis=0),
        everything,
        packed,
        doc_unit,
        jnp.broadcast_to(doc_factor, (own, lanes)),
        blank,
    )

    shares = dot(parts, passages, ((1,), (0,)))
    mixed = shares[:own] + mix(neg_rows, neg_scaled, slot_query)
    for steps in range(1, pool_size):
        mixed = mixed + forward(shares[steps * own : (steps + 1) * own], steps)
    total = lax.dynamic_slice(all_totals, (me, 0), (1, own)).reshape(own, 1)
    upstream = heat * (mixed / total - doc_unit)
    query_grad = back(query_factor, query_unit, upstream)
    return (objective, query_grad, document_grad, pool_grad)


def solution(mesh):
    rows = P(everyone, None)
    return jax.shard_map(
        local,
        mesh=mesh,
        in_specs=(rows, rows, rows, rows),
        out_specs=(P(), rows, rows, rows),
        check_vma=False,
    )
```

profile of v0, /device:TPU:1, one launch (start us, length us, event | category | flops | bytes accessed | tf_op | source)
XLA Modules:
  0.0 173.4 jit_solution(14544478653351944400)
XLA Ops:
  9.3 1.8 %multiply_reduce_fusion.1 = (f32[8]{0:T(128)S(1)}, f32[8,4096]{1,0:T(8,128)}, f32[8,4096]{1,0:T(8,128)S(1)}) fusion(f32[8,4096]{1,0:T(8,128)} %param.4, f32[8]{0:T(128)S(1)} %add_rsqrt_fusion, f32[8,4096]{1,0:T(8,128)} %param.5, f32[8]{0:T(128)S(1)} %add_rsqrt_fusion.1), kind=kLoop, calls=%fused_computation.40 | loop fusion | flops 131064 | bytes 524384 | tf_op jit(solution)/shard_map/reduce_sum | solution.py:421
  11.2 4.7 %collective-permute-start.4 = (f32[8,4096]{1,0:T(8,128)S(1)}, f32[8,4096]{1,0:T(8,128)S(1)}, u32[]{:S(2)}, u32[]{:S(2)}) collective-permute-start(f32[8,4096]{1,0:T(8,128)S(1)} %get-tuple-element.28.doc_unit), channel_id=1, source_target_pairs={{32,0},{36,4},{40,8},{44,12},{48,16},{52,20},{56,24},{60,28},{64,3... | collective-permute-start | bytes 393224 | tf_op jit(solution)/shard_map/ppermute | solution.py:359
  18.5 9.7 %all-to-all-start = ((s32[128,1,128]{2,1,0:T(1,128)}), s32[128,1,128]{2,1,0:T(1,128)S(1)}, u32[]{:S(2)}, u32[]{:S(2)}) async-start(s32[128,1,128]{2,1,0:T(1,128)} %bitcast.7), calls=%async_computation | async-start | bytes 131072 | tf_op jit(solution)/shard_map/all_to_all | solution.py:378
  29.0 2.7 %collective-permute-start.6 = (f32[32,4096]{1,0:T(8,128)S(1)}, f32[32,4096]{1,0:T(8,128)S(1)}, u32[]{:S(2)}, u32[]{:S(2)}) collective-permute-start(f32[32,4096]{1,0:T(8,128)S(1)} %pad_maximum_fusion.1.refs_0_), channel_id=1, source_target_pairs={{8,0},{12,4},{16,8},{20,12},{24,16},{28,20},{0,24},{4,28},{40,32},... | collective-permute-start | bytes 1572872 | tf_op jit(solution)/shard_map/ppermute | solution.py:359
  34.4 1.3 collective-permute-start.3
  35.6 2.5 %collective-permute-start.2 = (f32[8,4096]{1,0:T(8,128)S(1)}, f32[8,4096]{1,0:T(8,128)S(1)}, u32[]{:S(2)}, u32[]{:S(2)}) collective-permute-start(f32[8,4096]{1,0:T(8,128)S(1)} %broadcast_select_fusion.1), channel_id=1, source_target_pairs={{0,2},{1,3},{2,0},{3,1},{4,6},{5,7},{6,4},{7,5},{8,10},{9,11},{10,... | collective-permute-start | bytes 393224 | tf_op jit(solution)/shard_map/ppermute | solution.py:345
  38.1 1.1 collective-permute-start.1
  41.9 1.9 %collective-permute-done.2 = f32[8,4096]{1,0:T(8,128)S(1)} collective-permute-done((f32[8,4096]{1,0:T(8,128)S(1)}, f32[8,4096]{1,0:T(8,128)S(1)}, u32[]{:S(2)}, u32[]{:S(2)}) %collective-permute-start.2) | collective-permute-done | bytes 131104 | tf_op jit(solution)/shard_map/ppermute | solution.py:345
  45.3 7.2 %shard_map.75 = (f32[32,8,32,128]{3,2,1,0:T(8,128)}, f32[8,128]{1,0:T(8,128)}) custom-call(s32[128,128]{1,0:T(8,128)} %bitcast.37, f32[64,32,8,128]{3,2,1,0:T(8,128)} %bitcast.36, f32[32,4096]{1,0:T(8,128)} %copy-done.2, f32[32,4096]{1,0:T(8,128)} %pad_maximum_fusion.refs_1_), custom_call_target="tpu_custom_call" | custom-call | bytes 8388608 | tf_op jit(solution)/shard_map/pallas_call | solution.py:75
  52.5 10.5 %all-to-all-start.1 = ((f32[128,64,128]{2,1,0:T(8,128)}), f32[128,64,128]{2,1,0:T(8,128)}, u32[]{:S(2)}, u32[]{:S(2)}) async-start(f32[128,64,128]{2,1,0:T(8,128)} %bitcast.35), calls=%async_computation.1 | async-start | bytes 8388608 | tf_op jit(solution)/shard_map/all_to_all | solution.py:378
  66.2 1.1 collective-permute-start.9
  67.5 3.5 %shard_map.76.refs_1_.blank = f32[512,4096]{1,0:T(8,128)} custom-call(f32[8,128]{1,0:T(8,128)} %get-tuple-element.11._), custom_call_target="tpu_custom_call" | custom-call | bytes 8388608 | tf_op jit(solution)/shard_map/pallas_call | solution.py:105
  71.0 1.2 slice.55
  76.1 1.4 constant_dynamic-update-slice_fusion.7
  77.6 6.0 %fusion.36 = (f32[32]{0:T(128)S(1)}, f32[32,256]{1,0:T(8,128)S(1)}) fusion(f32[256,4096]{1,0:T(8,128)} %constant_dynamic-update-slice_fusion.7, f32[8,4096]{1,0:T(8,128)S(1)} %collective-permute-done.3, f32[8,4096]{1,0:T(8,128)S(1)} %collective-permute-done.2, f32[8,4096]{1,0:T(8,128)S(1)} %collective-permute-done.1, f32[8,4096]{1,0:T(8,128)S(1)} %broadcast_select_fusion.1), kind=kOutput, calls=%fused_computation.125 | convolution fusion | flops 403070944 | bytes 4751488 | tf_op jit(solution)/shard_map/dot_general | solution.py:335
  84.4 4.7 %fusion.37 = f32[32,4096]{1,0:T(8,128)S(1)} fusion(f32[32,256]{1,0:T(8,128)S(1)} %get-tuple-element.57, f32[256,4096]{1,0:T(8,128)} %constant_dynamic-update-slice_fusion.7), kind=kOutput, calls=%fused_computation.126 | convolution fusion | flops 402653184 | bytes 4751360 | tf_op jit(solution)/shard_map/dot_general | solution.py:335
  89.0 28.1 %all-to-all-done.1 = f32[128,64,128]{2,1,0:T(8,128)} async-done(((f32[128,64,128]{2,1,0:T(8,128)}), f32[128,64,128]{2,1,0:T(8,128)}, u32[]{:S(2)}, u32[]{:S(2)}) %all-to-all-start.1) | async-done | bytes 4194336 | tf_op jit(solution)/shard_map/all_to_all | solution.py:378
  117.9 7.0 %shard_map.77 = (f32[8,256]{1,0:T(8,128)}, f32[8,256]{1,0:T(8,128)}) custom-call(f32[32,8,32,128]{3,2,1,0:T(8,128)} %bitcast.12.packed, f32[8,4096]{1,0:T(8,128)} %get-tuple-element.27.unit, s32[1,256]{1,0:T(1,128)} %bitcast.48, s32[256,128]{1,0:T(8,128)} %broadcast_in_dim.145.named, f32[32]{0:T(128)} %copy-done.7, f32[512,4096]{1,0:T(8,128)} %shard_map.76.refs_1_.blank), custom_call_target="tpu_custom_call" | custom-call | flops 50331648 | bytes 4194304 | tf_op jit(solution)/shard_map/pallas_call | solution.py:155
  127.0 4.8 %all-to-all-start.2 = ((f32[128,1,306]{2,1,0:T(1,128)}), f32[128,1,306]{2,1,0:T(1,128)S(1)}, u32[]{:S(2)}, u32[]{:S(2)}) async-start(f32[128,1,306]{2,1,0:T(1,128)} %copy.45), calls=%async_computation.2 | async-start | bytes 393216 | tf_op jit(solution)/shard_map/all_to_all | solution.py:378
  131.8 2.7 %collective-permute-start.12 = (f32[8,4096]{1,0:T(8,128)S(1)}, f32[8,4096]{1,0:T(8,128)S(1)}, u32[]{:S(2)}, u32[]{:S(2)}) collective-permute-start(f32[8,4096]{1,0:T(8,128)S(1)} %get-tuple-element.32), channel_id=1, source_target_pairs={{0,3},{1,0},{2,1},{3,2},{4,7},{5,4},{6,5},{7,6},{8,11},{9,8},{10,9... | collective-permute-start | bytes 393224 | tf_op jit(solution)/shard_map/ppermute | solution.py:345
  135.6 4.9 %shard_map.78 = f32[8,4096]{1,0:T(8,128)} custom-call(f32[32,8,32,128]{3,2,1,0:T(8,128)} %bitcast.12.packed, f32[8,256]{1,0:T(8,128)} %get-tuple-element.13.scaled, s32[256,128]{1,0:T(8,128)} %broadcast_in_dim.145.named), custom_call_target="tpu_custom_call" | custom-call | flops 50331648 | bytes 4194304 | tf_op jit(solution)/shard_map/pallas_call | solution.py:194
  140.5 1.7 all-to-all-done.2
  146.0 1.1 select_maximum_fusion.weight
  148.8 16.6 %shard_map.79 = (f32[8,4096]{1,0:T(8,128)}, f32[512,4096]{1,0:T(8,128)}) custom-call(s32[1]{0:T(128)} %bitcast.17.count, s32[256]{0:T(256)} %get-tuple-element.19.slot_of, s32[256]{0:T(256)} %get-tuple-element.18.row_of, f32[272,1024]{1,0:T(8,128)} %select_maximum_fusion.weight, ...), custom_call_target="tpu_custom_call", output_to_operand_aliasing={{1}: (8, {})} | custom-call | flops 6845104128 | bytes 25165824 | tf_op jit(solution)/shard_map/pallas_call | solution.py:302
  (134 shorter events, 27.5 us)
Async XLA Ops:
  7.2 141.0 %all-gather.2.cloned.1.call-start = ((), (), s32[]{:S(2)}) async-start(), calls=%async_computation.3 | async-start | bytes 16908288 | tf_op jit(solution)/shard_map/all_gather | solution.py:398
  11.2 136.0 %copy-start.1 = (f32[8,4096]{1,0:T(8,128)}, f32[8,4096]{1,0:T(8,128)S(1)}, u32[]{:S(2)}) copy-start(f32[8,4096]{1,0:T(8,128)S(1)} %get-tuple-element.28.doc_unit) | copy-start | bytes 393220
  11.2 17.8 %collective-permute-start.4 = (f32[8,4096]{1,0:T(8,128)S(1)}, f32[8,4096]{1,0:T(8,128)S(1)}, u32[]{:S(2)}, u32[]{:S(2)}) collective-permute-start(f32[8,4096]{1,0:T(8,128)S(1)} %get-tuple-element.28.doc_unit), channel_id=1, source_target_pairs={{32,0},{36,4},{40,8},{44,12},{48,16},{52,20},{56,24},{60,28},{64,3... | collective-permute-start | bytes 393224 | tf_op jit(solution)/shard_map/ppermute | solution.py:359
  15.8 13.1 %collective-permute-start.5 = (f32[8,4096]{1,0:T(8,128)S(1)}, f32[8,4096]{1,0:T(8,128)S(1)}, u32[]{:S(2)}, u32[]{:S(2)}) collective-permute-start(f32[8,4096]{1,0:T(8,128)S(1)} %get-tuple-element.28.doc_unit), channel_id=1, source_target_pairs={{64,0},{68,4},{72,8},{76,12},{80,16},{84,20},{88,24},{92,28},{96,3... | collective-permute-start | bytes 393224 | tf_op jit(solution)/shard_map/ppermute | solution.py:359
  15.8 13.1 %collective-permute-start = (f32[8,4096]{1,0:T(8,128)S(1)}, f32[8,4096]{1,0:T(8,128)S(1)}, u32[]{:S(2)}, u32[]{:S(2)}) collective-permute-start(f32[8,4096]{1,0:T(8,128)S(1)} %get-tuple-element.28.doc_unit), channel_id=1, source_target_pairs={{96,0},{100,4},{104,8},{108,12},{112,16},{116,20},{120,24},{124,28... | collective-permute-start | bytes 393224 | tf_op jit(solution)/shard_map/ppermute | solution.py:359
  18.5 26.2 %all-to-all-start = ((s32[128,1,128]{2,1,0:T(1,128)}), s32[128,1,128]{2,1,0:T(1,128)S(1)}, u32[]{:S(2)}, u32[]{:S(2)}) async-start(s32[128,1,128]{2,1,0:T(1,128)} %bitcast.7), calls=%async_computation | async-start | bytes 131072 | tf_op jit(solution)/shard_map/all_to_all | solution.py:378
  29.0 15.7 %copy-start.2 = (f32[32,4096]{1,0:T(8,128)}, f32[32,4096]{1,0:T(8,128)S(1)}, u32[]{:S(2)}) copy-start(f32[32,4096]{1,0:T(8,128)S(1)} %pad_maximum_fusion.1.refs_0_) | copy-start | bytes 1572868
  29.0 34.0 %collective-permute-start.6 = (f32[32,4096]{1,0:T(8,128)S(1)}, f32[32,4096]{1,0:T(8,128)S(1)}, u32[]{:S(2)}, u32[]{:S(2)}) collective-permute-start(f32[32,4096]{1,0:T(8,128)S(1)} %pad_maximum_fusion.1.refs_0_), channel_id=1, source_target_pairs={{8,0},{12,4},{16,8},{20,12},{24,16},{28,20},{0,24},{4,28},{40,32},... | collective-permute-start | bytes 1572872 | tf_op jit(solution)/shard_map/ppermute | solution.py:359
  31.7 32.4 %collective-permute-start.7 = (f32[32,4096]{1,0:T(8,128)S(1)}, f32[32,4096]{1,0:T(8,128)S(1)}, u32[]{:S(2)}, u32[]{:S(2)}) collective-permute-start(f32[32,4096]{1,0:T(8,128)S(1)} %pad_maximum_fusion.1.refs_0_), channel_id=1, source_target_pairs={{16,0},{20,4},{24,8},{28,12},{0,16},{4,20},{8,24},{12,28},{48,32},... | collective-permute-start | bytes 1572872 | tf_op jit(solution)/shard_map/ppermute | solution.py:359
  34.4 7.0 %collective-permute-start.3 = (f32[8,4096]{1,0:T(8,128)S(1)}, f32[8,4096]{1,0:T(8,128)S(1)}, u32[]{:S(2)}, u32[]{:S(2)}) collective-permute-start(f32[8,4096]{1,0:T(8,128)S(1)} %broadcast_select_fusion.1), channel_id=1, source_target_pairs={{0,1},{1,2},{2,3},{3,0},{4,5},{5,6},{6,7},{7,4},{8,9},{9,10},{10,1... | collective-permute-start | bytes 393224 | tf_op jit(solution)/shard_map/ppermute | solution.py:345
  35.6 8.2 %collective-permute-start.2 = (f32[8,4096]{1,0:T(8,128)S(1)}, f32[8,4096]{1,0:T(8,128)S(1)}, u32[]{:S(2)}, u32[]{:S(2)}) collective-permute-start(f32[8,4096]{1,0:T(8,128)S(1)} %broadcast_select_fusion.1), channel_id=1, source_target_pairs={{0,2},{1,3},{2,0},{3,1},{4,6},{5,7},{6,4},{7,5},{8,10},{9,11},{10,... | collective-permute-start | bytes 393224 | tf_op jit(solution)/shard_map/ppermute | solution.py:345
  38.1 5.8 %collective-permute-start.1 = (f32[8,4096]{1,0:T(8,128)S(1)}, f32[8,4096]{1,0:T(8,128)S(1)}, u32[]{:S(2)}, u32[]{:S(2)}) collective-permute-start(f32[8,4096]{1,0:T(8,128)S(1)} %broadcast_select_fusion.1), channel_id=1, source_target_pairs={{0,3},{1,0},{2,1},{3,2},{4,7},{5,4},{6,5},{7,6},{8,11},{9,8},{10,9... | collective-permute-start | bytes 393224 | tf_op jit(solution)/shard_map/ppermute | solution.py:345
  41.3 23.8 %collective-permute-start.8 = (f32[32,4096]{1,0:T(8,128)S(1)}, f32[32,4096]{1,0:T(8,128)S(1)}, u32[]{:S(2)}, u32[]{:S(2)}) collective-permute-start(f32[32,4096]{1,0:T(8,128)S(1)} %pad_maximum_fusion.1.refs_0_), channel_id=1, source_target_pairs={{24,0},{28,4},{0,8},{4,12},{8,16},{12,20},{16,24},{20,28},{56,32},... | collective-permute-start | bytes 1572872 | tf_op jit(solution)/shard_map/ppermute | solution.py:359
  52.5 64.7 %all-to-all-start.1 = ((f32[128,64,128]{2,1,0:T(8,128)}), f32[128,64,128]{2,1,0:T(8,128)}, u32[]{:S(2)}, u32[]{:S(2)}) async-start(f32[128,64,128]{2,1,0:T(8,128)} %bitcast.35), calls=%async_computation.1 | async-start | bytes 8388608 | tf_op jit(solution)/shard_map/all_to_all | solution.py:378
  66.2 9.9 %collective-permute-start.9 = (f32[128,4096]{1,0:T(8,128)}, f32[128,4096]{1,0:T(8,128)S(1)}, u32[]{:S(2)}, u32[]{:S(2)}) collective-permute-start(f32[128,4096]{1,0:T(8,128)} %get-tuple-element.34), channel_id=1, source_target_pairs={{4,0},{0,4},{12,8},{8,12},{20,16},{16,20},{28,24},{24,28},{36,32},... | collective-permute-start | bytes 6291464 | tf_op jit(solution)/shard_map/ppermute | solution.py:359
  67.5 49.7 %copy-start.6 = (s32[256]{0:T(256)}, s32[256]{0:T(256)S(1)}, u32[]{:S(2)}) copy-start(s32[256]{0:T(256)S(1)} %broadcast_add_fusion) | copy-start | bytes 3076
  67.5 5.3 %copy-start.4 = (s32[128,1,128]{2,1,0:T(1,128)S(1)}, s32[128,1,128]{2,1,0:T(1,128)}, u32[]{:S(2)}) copy-start(s32[128,1,128]{2,1,0:T(1,128)} %copy-done.3) | copy-start | bytes 196612
  83.6 34.3 %copy-start.7 = (f32[32]{0:T(128)}, f32[32]{0:T(128)S(1)}, u32[]{:S(2)}) copy-start(f32[32]{0:T(128)S(1)} %get-tuple-element.56.refs_0_) | copy-start | bytes 388
  127.0 15.2 %all-to-all-start.2 = ((f32[128,1,306]{2,1,0:T(1,128)}), f32[128,1,306]{2,1,0:T(1,128)S(1)}, u32[]{:S(2)}, u32[]{:S(2)}) async-start(f32[128,1,306]{2,1,0:T(1,128)} %copy.45), calls=%async_computation.2 | async-start | bytes 393216 | tf_op jit(solution)/shard_map/all_to_all | solution.py:378
  131.8 15.3 %collective-permute-start.12 = (f32[8,4096]{1,0:T(8,128)S(1)}, f32[8,4096]{1,0:T(8,128)S(1)}, u32[]{:S(2)}, u32[]{:S(2)}) collective-permute-start(f32[8,4096]{1,0:T(8,128)S(1)} %get-tuple-element.32), channel_id=1, source_target_pairs={{0,3},{1,0},{2,1},{3,2},{4,7},{5,4},{6,5},{7,6},{8,11},{9,8},{10,9... | collective-permute-start | bytes 393224 | tf_op jit(solution)/shard_map/ppermute | solution.py:345
  134.5 12.6 %collective-permute-start.11 = (f32[8,4096]{1,0:T(8,128)S(1)}, f32[8,4096]{1,0:T(8,128)S(1)}, u32[]{:S(2)}, u32[]{:S(2)}) collective-permute-start(f32[8,4096]{1,0:T(8,128)S(1)} %get-tuple-element.33), channel_id=1, source_target_pairs={{0,2},{1,3},{2,0},{3,1},{4,6},{5,7},{6,4},{7,5},{8,10},{9,11},{10,... | collective-permute-start | bytes 393224 | tf_op jit(solution)/shard_map/ppermute | solution.py:345
  135.0 12.1 %collective-permute-start.10 = (f32[8,4096]{1,0:T(8,128)S(1)}, f32[8,4096]{1,0:T(8,128)S(1)}, u32[]{:S(2)}, u32[]{:S(2)}) collective-permute-start(f32[8,4096]{1,0:T(8,128)S(1)} %get-tuple-element.31), channel_id=1, source_target_pairs={{0,1},{1,2},{2,3},{3,0},{4,5},{5,6},{6,7},{7,4},{8,9},{9,10},{10,1... | collective-permute-start | bytes 393224 | tf_op jit(solution)/shard_map/ppermute | solution.py:345
  140.5 6.6 %copy-start = (f32[8,4096]{1,0:T(8,128)S(1)}, f32[8,4096]{1,0:T(8,128)}, u32[]{:S(2)}) copy-start(f32[8,4096]{1,0:T(8,128)} %get-tuple-element.27.unit) | copy-start | bytes 393220
  140.5 6.6 %copy-start.5 = (f32[8,4096]{1,0:T(8,128)S(1)}, f32[8,4096]{1,0:T(8,128)}, u32[]{:S(2)}) copy-start(f32[8,4096]{1,0:T(8,128)} %shard_map.78) | copy-start | bytes 393220
  (1 other events, 0.6 us)
Sparse Core Ops, SparseCore 0:
  11.7 128.7 all-gather.1
where the time goes:
time: 174 us; the launch traced here: 173 us
  starting transfers between devices  44.1 us (25%)
  Pallas kernels  39.1 us (22%)
  waiting for transfers between devices  31.8 us (18%)
  between operations  17.7 us (10%)
  local copies, waits for them, and re-layouts  16.9 us (10%)
  other arithmetic  12.2 us (7%)
  matrix products  11.6 us (7%)
    all_to_all x3, waiting for transfers between devices, exchange(): lax.all_to_all(values, everyone, split_axis=0, concat_axis=0, tiled=True)  29.8 us
    all_to_all x3, starting transfers between devices, exchange(): lax.all_to_all(values, everyone, split_axis=0, concat_axis=0, tiled=True)  25 us
    pallas_call x1, Pallas kernels, finish(): pl.pallas_call(finish_kernel, in_specs=[smem, smem, smem, vmem, anywhere,...  16.6 us
    dot_general x3, matrix products, dot(): lax.dot_general(left, right, (contract, ((), ())), precision=highest, pre...  11.6 us
    ppermute x7, starting transfers between devices, ahead(): blocks.append(lax.ppermute(values, 'dp', pairs))  10.3 us
    ppermute x6, starting transfers between devices, forward(): lax.ppermute(values, 'pool', [(i, (i + steps) % 4) for i in range(4)])  8.66 us
    pallas_call x1, Pallas kernels, pick(): pl.pallas_call(functools.partial(pick_kernel, own), in_specs=[pl.BlockSpe...  7.15 us
    pallas_call x1, Pallas kernels, against(): pl.pallas_call(against_kernel, in_specs=[anywhere, vmem, vmem, vmem] + [a...  7.02 us
  transfers between devices with their start and end apart: 17, of which 3 were waited for; matrix products, arithmetic and copies ran while one was open for 20% of the time, Pallas kernels for 13%

commit v1 on v0

--- a/solution.py
+++ b/solution.py
@@ -108,8 +108,45 @@
         out_specs=pl.BlockSpec(memory_space=pl.ANY),
         out_shape=jax.ShapeDtypeStruct((rows, width), jnp.float32),
         scratch_shapes=[pltpu.VMEM((step, width), jnp.float32), pltpu.SemaphoreType.DMA((rows // step,))],
-        cost_estimate=pl.CostEstimate(flops=0, bytes_accessed=4 * rows * width, transcendentals=0),
     )(earlier)
+
+
+def beside_kernel(queries, documents, parts, shares):
+    step = 8 * lanes
+    width = queries.shape[1]
+    query_squares = jnp.zeros((queries.shape[0], lanes), jnp.float32)
+    doc_squares = jnp.zeros((documents.shape[0], lanes), jnp.float32)
+    scores = jnp.zeros(parts.shape, jnp.float32)
+    for i in range(width // step):
+        query, document = (a[:, i * step : (i + 1) * step] for a in (queries, documents))
+        for j in range(step // lanes):
+            columns = slice(j * lanes, (j + 1) * lanes)
+            query_squares = query_squares + query[:, columns] * query[:, columns]
+            doc_squares = doc_squares + document[:, columns] * document[:, columns]
+        scores = scores + dot3(halves(query), halves(document), ((1,), (1,)))
+    query_scale = lax.rsqrt(jnp.sum(query_squares, axis=1, keepdims=True) + epsilon)
+    doc_scale = lax.rsqrt(jnp.sum(doc_squares, axis=1, keepdims=True) + epsilon)
+    doc_scale = jnp.transpose(jnp.broadcast_to(doc_scale, doc_squares.shape))[: parts.shape[0]]
+    chosen = jnp.exp(heat * (scores * (query_scale * doc_scale)) - heat)
+    parts[...] = chosen
+    left = halves(chosen * doc_scale)
+    for i in range(width // step):
+        columns = slice(i * step, (i + 1) * step)
+        shares[:, columns] = dot3(left, halves(documents[:, columns]), ((1,), (0,)))
+
+
+def beside(queries, documents):
+    vmem = pl.BlockSpec(memory_space=pltpu.VMEM)
+    return pl.pallas_call(
+        beside_kernel,
+        in_specs=[vmem, vmem],
+        out_specs=[vmem, vmem],
+        out_shape=[
+            jax.ShapeDtypeStruct((queries.shape[0], documents.shape[0]), jnp.float32),
+            jax.ShapeDtypeStruct(queries.shape, jnp.float32),
+        ],
+        compiler_params=pltpu.CompilerParams(vmem_limit_bytes=limit),
+    )(queries, documents)
 
 
 def row_fetches(packed, tiles, came, i, step):
@@ -117,14 +154,21 @@
     return [pltpu.make_async_copy(packed.at[:, s, part], tiles.at[:, part, s], came.at[i, s]) for s in range(8)]
 
 
-def against_kernel(packed, unit, asker, named, *refs):
-    parts, scaled, tiles, came = refs[-4:]
+def against_kernel(packed, queries, documents, asker, named, *refs):
+    parts, scaled, facts, tiles, came = refs[-5:]
     own, count = parts.shape
     strips = tiles.shape[1]
     step = 8
     for i in range(strips // step):
         for fetch in row_fetches(packed, tiles, came, i, step):
             fetch.start()
+    query, document = queries[...], documents[...]
+    query_scale = lax.rsqrt(jnp.sum(query * query, axis=1, keepdims=True) + epsilon)
+    doc_scale = lax.rsqrt(jnp.sum(document * document, axis=1, keepdims=True) + epsilon)
+    unit = query * query_scale
+    diagonal = heat * jnp.sum(unit * (document * doc_scale), axis=1, keepdims=True)
+    lane = lax.broadcasted_iota(jnp.int32, facts.shape, 1)
+    facts[...] = jnp.where(lane == 0, query_scale, jnp.where(lane == 1, doc_scale, diagonal))
     real = named[...] >= 0
     scores = jnp.zeros((own, count), jnp.float32)
     squares = jnp.zeros((count, lanes), jnp.float32)
@@ -147,16 +191,17 @@
     scaled[...] = chosen * scale
 
 
-def against(packed, unit, asker, *earlier):
-    own, width = unit.shape
+def against(packed, queries, documents, asker, *earlier):
+    own, width = queries.shape
     groups = packed.shape[0]
     vmem = pl.BlockSpec(memory_space=pltpu.VMEM)
     anywhere = pl.BlockSpec(memory_space=pl.ANY)
     return pl.pallas_call(
         against_kernel,
-        in_specs=[anywhere, vmem, vmem, vmem] + [anywhere] * len(earlier),
-        out_specs=[vmem, vmem],
-        out_shape=[jax.ShapeDtypeStruct((own, 8 * groups), jnp.float32)] * 2,
+        in_specs=[anywhere, vmem, vmem, vmem, vmem] + [anywhere] * len(earlier),
+        out_specs=[vmem, vmem, vmem],
+        out_shape=[jax.ShapeDtypeStruct((own, 8 * groups), jnp.float32)] * 2
+        + [jax.ShapeDtypeStruct((own, lanes), jnp.float32)],
         scratch_shapes=[
             pltpu.VMEM((groups, width // lanes, 8, lanes), jnp.float32),
             pltpu.SemaphoreType.DMA((width // lanes // 8, 8)),
@@ -165,7 +210,7 @@
         cost_estimate=pl.CostEstimate(
             flops=48 * own * groups * width, bytes_accessed=32 * width * groups, transcendentals=0
         ),
-    )(packed, unit, asker[None, :], jnp.broadcast_to(asker[:, None], (8 * groups, lanes)), *earlier)
+    )(packed, queries, documents, asker[None, :], jnp.broadcast_to(asker[:, None], (8 * groups, lanes)), *earlier)
 
 
 def mix_kernel(packed, scaled, named, mixed, tiles, came):
@@ -209,31 +254,38 @@
 
 def finish_kernel(
     count, slot_of, row_of, weight, queries, packed, doc_unit, doc_factor, blank,
-    doc_grad, pool_grad, held, tiles, upstream, inner, squares, high, low, query_sem, came, row_sem,
+    doc_grad, pool_grad, held, tiles, upstream, inner, squares, given, both, query_sem, came, row_sem, given_sem,
 ):
     slots = inner.shape[0]
     width = queries.shape[1]
     own = doc_unit.shape[0]
-    step = 4
+    step = 8
     block = step * lanes
 
     def query_copy(i):
         columns = pl.ds(i * block, block)
         return pltpu.make_async_copy(queries.at[:, columns], held.at[:, columns], query_sem.at[i])
 
+    give = pltpu.make_async_copy(weight, given, given_sem)
+    give.start()
     for i in range(width // block):
         query_copy(i).start()
         for fetch in row_fetches(packed, tiles, came, i, step):
             fetch.start()
-    first, second = halves(weight[...])
-    high[...] = first
-    low[...] = second
+    give.wait()
+    total = given.shape[0]
+    first, second = halves(given[...])
+    both[:total] = first
+    both[total:] = second
     inner[...] = jnp.zeros_like(inner)
     squares[...] = jnp.zeros_like(squares)
     for i in range(width // block):
         columns = slice(i * block, (i + 1) * block)
         query_copy(i).wait()
-        above = dot3((high[...], low[...]), halves(held[:, columns]), ((1,), (0,)))
+        high, low = halves(held[:, columns])
+        twice = jnp.dot(both[...], high, preferred_element_type=jnp.float32)
+        once = jnp.dot(both[:total], low, preferred_element_type=jnp.float32)
+        above = twice[:total] + (once + twice[total:])
         upstream[:, columns] = above
         for fetch in row_fetches(packed, tiles, came, i, step):
             fetch.wait()
@@ -293,7 +345,7 @@
     slots = 8 * groups
     own, width = doc_unit.shape
     batch = queries.shape[0]
-    steps = strips // 4
+    steps = strips // 8
     total = slots + 2 * own
     weight = jnp.pad(weight, ((0, total - weight.shape[0]), (0, 0)))
     vmem = pl.BlockSpec(memory_space=pltpu.VMEM)
@@ -301,7 +353,7 @@
     smem = pl.BlockSpec(memory_space=pltpu.SMEM)
     return pl.pallas_call(
         finish_kernel,
-        in_specs=[smem, smem, smem, vmem, anywhere, anywhere, vmem, vmem, anywhere],
+        in_specs=[smem, smem, smem, anywhere, anywhere, anywhere, vmem, vmem, anywhere],
         out_specs=[vmem, anywhere],
         scratch_shapes=[
             pltpu.VMEM((batch, width), jnp.float32),
@@ -309,10 +361,11 @@
             pltpu.VMEM((total, width), jnp.float32),
             pltpu.VMEM((slots, lanes), jnp.float32),
             pltpu.VMEM((slots, lanes), jnp.float32),
-            pltpu.VMEM((total, batch), jnp.bfloat16),
-            pltpu.VMEM((total, batch), jnp.bfloat16),
+            pltpu.VMEM((total, batch), jnp.float32),
+            pltpu.VMEM((2 * total, batch), jnp.bfloat16),
             pltpu.SemaphoreType.DMA((steps,)),
             pltpu.SemaphoreType.DMA((steps, 8)),
+            pltpu.SemaphoreType.DMA,
             pltpu.SemaphoreType.DMA,
         ],
         out_shape=[
@@ -341,8 +394,15 @@
     return factor * (upstream - unit * jnp.sum(unit * upstream, axis=-1, keepdims=True))
 
 
-def forward(values, steps):
-    return lax.ppermute(values, "pool", [(i, (i + steps) % 4) for i in range(4)])
+def swap(values, bits):
+    return lax.ppermute(values, "pool", [(i, i ^ bits) for i in range(4)])
+
+
+def by_index(values, member):
+    values = values.reshape((2, 2) + values.shape[1:]).swapaxes(0, 1)
+    values = jnp.where(member // 2 == 1, values[::-1], values)
+    values = jnp.where(member % 2 == 1, values[:, ::-1], values)
+    return values.reshape((4,) + values.shape[2:])
 
 
 def ahead(values, direction, size):
@@ -391,17 +451,10 @@
     request = jnp.pad(request, ((0, 0), (0, lanes - capacity)), constant_values=-1)
     asked = exchange(request)
 
-    doc_factor = factor_of(documents)
-    doc_unit = documents * doc_factor
-    query_factor = factor_of(queries)
-    query_unit = queries * query_factor
-    everything = lax.all_gather(query_unit, everyone, axis=0, tiled=True)
-    passages = ahead(doc_unit, (1, 0, 0), 4)
-
-    cohort = jnp.where(passages[-1, 0] >= -2.0, query_unit, 0.0)
-    cohort = jnp.concatenate(
-        [cohort] + [forward(cohort, -steps) for steps in range(1, pool_size)], axis=0
-    )
+    everything = lax.all_gather(queries, everyone, axis=0, tiled=True)
+    passages = ahead(documents, (1, 0, 0), 4)
+    cohort = jnp.concatenate([queries, swap(queries, 2)], axis=0)
+    cohort = jnp.concatenate([cohort, swap(cohort, 1)], axis=0)
     packed, done = pick(asked, own, document_pool, passages, cohort)
     neg_rows = exchange(packed.reshape(devices, capacity * strips, lanes)).reshape(packed.shape)
 
@@ -413,26 +466,29 @@
     blank = clear(pool_rows, width, done)
 
     passages = ahead(ahead(passages, (0, 1, 0), 4), (0, 0, 1), 2)
-    parts = jnp.exp(heat * dot(cohort, passages, ((1,), (1,))) - heat)
+    parts, shares = beside(cohort, passages)
     sums = jnp.sum(parts, axis=1)
 
-    neg_parts, neg_scaled = against(neg_rows, query_unit, slot_query, sums, blank)
-
-    diagonal = heat * jnp.sum(query_unit * doc_unit, axis=1)
-    block = jnp.roll(parts.reshape(pool_size, own, groups * own), member, axis=0)
+    neg_parts, neg_scaled, facts = against(neg_rows, queries, documents, slot_query, sums, blank)
+    query_factor, doc_factor, diagonal = facts[:, 0:1], facts[:, 1:2], facts[:, 2]
+    query_unit = queries * query_factor
+    doc_unit = documents * doc_factor
+
+    block = by_index(parts.reshape(pool_size, own, groups * own), member)
     block = block.reshape(own * pool_size, groups * own).T.reshape(2, 4, 4, own, own * pool_size)
     block = block.transpose(2, 1, 0, 3, 4)
     for axis, index in enumerate((me // 32, me // 8 % 4, me // 4 % 2)):
         block = jnp.roll(block, index, axis=axis)
     block = block.reshape(groups, 1, -1)
     here = jnp.arange(pool_size, dtype=jnp.int32)[None, :, None] == member
-    sums = jnp.roll(sums.reshape(pool_size, own), member, axis=0).reshape(-1)
+    sums = by_index(sums.reshape(pool_size, own), member).reshape(-1)
     news = jnp.concatenate(
         [
             jnp.where(here, block, 0.0).reshape(devices, -1),
             jnp.broadcast_to(sums, (devices, own * pool_size)),
             jnp.broadcast_to(jnp.sum(neg_parts, axis=1), (devices, own)),
             jnp.broadcast_to(diagonal, (devices, own)),
+            jnp.broadcast_to(query_factor.reshape(1, own), (devices, own)),
             jnp.sum(neg_parts, axis=0).reshape(devices, capacity),
         ],
         axis=1,
@@ -444,13 +500,14 @@
     doc_parts = both[:, :edge].reshape(groups, own, own * pool_size).transpose(1, 0, 2)
     all_totals = both[:, edge:].reshape(devices, own) + news[:, shared : shared + own]
     all_diagonal = news[:, shared + own : shared + 2 * own]
-    slot_parts = news[:, shared + 2 * own :].reshape(-1)
+    all_factors = news[:, shared + 2 * own : shared + 3 * own].reshape(1, batch)
+    slot_parts = news[:, shared + 3 * own :].reshape(-1)
     objective = jnp.sum(jnp.log(all_totals) + heat - all_diagonal) / batch
 
-    scale = heat / all_totals.reshape(1, batch)
+    scale = heat * all_factors / all_totals.reshape(1, batch)
     number = jnp.arange(batch, dtype=jnp.int32)[None, :]
     matched = number == me * own + jnp.arange(own, dtype=jnp.int32)[:, None]
-    doc_weight = doc_parts.reshape(own, batch) * scale - heat * matched.astype(jnp.float32)
+    doc_weight = doc_parts.reshape(own, batch) * scale - jnp.where(matched, heat * all_factors, 0.0)
     slot_order = jnp.arange(slots, dtype=jnp.int32)
     spread = jnp.where(place[:, None] == number, slot_parts[:, None], 0.0)
     same = (named_row[:, None] == named_row[None, :]) & valid[None, :]
@@ -473,10 +530,9 @@
         blank,
     )
 
-    shares = dot(parts, passages, ((1,), (0,)))
     mixed = shares[:own] + mix(neg_rows, neg_scaled, slot_query)
-    for steps in range(1, pool_size):
-        mixed = mixed + forward(shares[steps * own : (steps + 1) * own], steps)
+    for i, bits in ((1, 2), (2, 1), (3, 3)):
+        mixed = mixed + swap(shares[i * own : (i + 1) * own], bits)
     total = lax.dynamic_slice(all_totals, (me, 0), (1, own)).reshape(own, 1)
     upstream = heat * (mixed / total - doc_unit)
     query_grad = back(query_factor, query_unit, upstream)

time: 174 us -> 175 us (level)
  matrix products: 11.6 us -> 0.89 us
  Pallas kernels: 39.1 us -> 48.5 us
  waiting for transfers between devices: 31.8 us -> 40.1 us
  other arithmetic: 12.2 us -> 8 us
  starting transfers between devices: 44.1 us -> 40.4 us
  local copies, waits for them, and re-layouts: 16.9 us -> 20.5 us
    dot_general x3 -> x1, matrix products: 11.6 us -> 0.89 us  [dot(): lax.dot_general(left, right, (contract, ((), ())), precision=highest, pre...]
    pallas_call x2 -> x3, Pallas kernels: 23.6 us -> 32.2 us  [the longest x1 17.8 us: finish(): pl.pallas_call(finish_kernel, in_specs=[smem, smem, smem, anywhere, anywh...]
    all_to_all x3, starting transfers between devices: 25 us -> 19.7 us  [exchange(): lax.all_to_all(values, everyone, split_axis=0, concat_axis=0, tiled=True)]
    ppermute x6 -> x5, waiting for transfers between devices: 1.96 us -> 5.41 us  [swap(): return lax.ppermute(values, 'pool', [(i, i ^ bits) for i in range(4)])]
    all_to_all x3, waiting for transfers between devices: 29.8 us -> 33.1 us  [exchange(): lax.all_to_all(values, everyone, split_axis=0, concat_axis=0, tiled=True)]
    reduce_sum x3 -> x1, other arithmetic: 3.93 us -> 0.87 us  [local(): sums = jnp.sum(parts, axis=1)]
    ppermute x7, starting transfers between devices: 10.3 us -> 12.7 us  [ahead(): blocks.append(lax.ppermute(values, 'dp', pairs))]
    unnamed x22 -> x30, local copies, waits for them, and re-layouts: 5.62 us -> 7.65 us
  transfers between devices with their start and end apart: 17 -> 16, of which waited for: 3 -> 4; matrix products, arithmetic and copies ran while one was open for 20% -> 16% of each run, Pallas kernels for 13% -> 17%
where the time goes in v1:
time: 175 us
  Pallas kernels  48.5 us (28%)
  starting transfers between devices  40.4 us (23%)
  waiting for transfers between devices  40.1 us (23%)
  local copies, waits for them, and re-layouts  20.5 us (12%)
  between operations  17.1 us (10%)
  other arithmetic  8 us (5%)
    all_to_all x3, waiting for transfers between devices, exchange(): lax.all_to_all(values, everyone, split_axis=0, concat_axis=0, tiled=True)  33.1 us
    all_to_all x3, starting transfers between devices, exchange(): lax.all_to_all(values, everyone, split_axis=0, concat_axis=0, tiled=True)  19.7 us
    pallas_call x1, Pallas kernels, finish(): pl.pallas_call(finish_kernel, in_specs=[smem, smem, smem, anywhere, anywh...  17.8 us
    ppermute x7, starting transfers between devices, ahead(): blocks.append(lax.ppermute(values, 'dp', pairs))  12.7 us
    ppermute x5, starting transfers between devices, swap(): return lax.ppermute(values, 'pool', [(i, i ^ bits) for i in range(4)])  8.04 us
    pallas_call x1, Pallas kernels, pick(): pl.pallas_call(functools.partial(pick_kernel, own), in_specs=[pl.BlockSpe...  7.88 us
    unnamed x30, local copies, waits for them, and re-layouts  7.65 us
    pallas_call x1, Pallas kernels, beside(): pl.pallas_call(beside_kernel, in_specs=[vmem, vmem], out_specs=[vmem, vme...  7.55 us
  transfers between devices with their start and end apart: 16, of which 4 were waited for; matrix products, arithmetic and copies ran while one was open for 16% of the time, Pallas kernels for 17%

profile of v1, /device:TPU:1, one launch (start us, length us, event | category | flops | bytes accessed | tf_op | source)
XLA Modules:
  0.0 175.4 jit_solution(7629794062652013325)
XLA Ops:
  7.9 2.5 %collective-permute-start.4 = (f32[8,4096]{1,0:T(8,128)}, f32[8,4096]{1,0:T(8,128)S(1)}, u32[]{:S(2)}, u32[]{:S(2)}) collective-permute-start(f32[8,4096]{1,0:T(8,128)} %documents.1), channel_id=1, source_target_pairs={{96,0},{100,4},{104,8},{108,12},{112,16},{116,20},{120,24},{124,28... | collective-permute-start | bytes 393224 | tf_op jit(solution)/shard_map/ppermute | solution.py:419
  10.4 3.3 %collective-permute-start.3 = (f32[8,4096]{1,0:T(8,128)}, f32[8,4096]{1,0:T(8,128)S(1)}, u32[]{:S(2)}, u32[]{:S(2)}) collective-permute-start(f32[8,4096]{1,0:T(8,128)} %documents.1), channel_id=1, source_target_pairs={{64,0},{68,4},{72,8},{76,12},{80,16},{84,20},{88,24},{92,28},{96,3... | collective-permute-start | bytes 393224 | tf_op jit(solution)/shard_map/ppermute | solution.py:419
  14.5 2.9 %collective-permute-start = (f32[8,4096]{1,0:T(8,128)}, f32[8,4096]{1,0:T(8,128)S(1)}, u32[]{:S(2)}, u32[]{:S(2)}) collective-permute-start(f32[8,4096]{1,0:T(8,128)} %queries.1), channel_id=1, source_target_pairs={{0,2},{1,3},{2,0},{3,1},{4,6},{5,7},{6,4},{7,5},{8,10},{9,11},{10,... | collective-permute-start | bytes 393224 | tf_op jit(solution)/shard_map/ppermute | solution.py:398
  19.3 6.6 %all-to-all-start = ((s32[128,1,128]{2,1,0:T(1,128)}), s32[128,1,128]{2,1,0:T(1,128)S(1)}, u32[]{:S(2)}, u32[]{:S(2)}) async-start(s32[128,1,128]{2,1,0:T(1,128)} %bitcast.8), calls=%async_computation | async-start | bytes 131072 | tf_op jit(solution)/shard_map/all_to_all | solution.py:438
  26.0 1.6 constant_dynamic-update-slice_fusion.13
  30.7 1.4 collective-permute-start.7
  32.1 2.4 %collective-permute-start.6 = (f32[32,4096]{1,0:T(8,128)S(1)}, f32[32,4096]{1,0:T(8,128)S(1)}, u32[]{:S(2)}, u32[]{:S(2)}) collective-permute-start(f32[32,4096]{1,0:T(8,128)S(1)} %get-tuple-element.50.refs_0_), channel_id=1, source_target_pairs={{16,0},{20,4},{24,8},{28,12},{0,16},{4,20},{8,24},{12,28},{48,32},... | collective-permute-start | bytes 1572872 | tf_op jit(solution)/shard_map/ppermute | solution.py:419
  34.5 1.2 collective-permute-start.5
  35.7 1.3 collective-permute-start.1
  36.9 5.4 %collective-permute-done.1 = f32[16,4096]{1,0:T(8,128)S(1)} collective-permute-done((f32[16,4096]{1,0:T(8,128)S(1)}, f32[16,4096]{1,0:T(8,128)S(1)}, u32[]{:S(2)}, u32[]{:S(2)}) %collective-permute-start.1) | collective-permute-done | bytes 262176 | tf_op jit(solution)/shard_map/ppermute | solution.py:398
  43.2 7.9 %shard_map.76 = (f32[32,8,32,128]{3,2,1,0:T(8,128)}, f32[8,128]{1,0:T(8,128)}) custom-call(s32[128,128]{1,0:T(8,128)} %bitcast.37, f32[64,32,8,128]{3,2,1,0:T(8,128)} %bitcast.36, f32[32,4096]{1,0:T(8,128)} %copy-done.6, f32[32,4096]{1,0:T(8,128)} %copy-done.2), custom_call_target="tpu_custom_call" | custom-call | bytes 8388608 | tf_op jit(solution)/shard_map/pallas_call | solution.py:75
  51.1 8.7 %all-to-all-start.1 = ((f32[128,64,128]{2,1,0:T(8,128)}), f32[128,64,128]{2,1,0:T(8,128)}, u32[]{:S(2)}, u32[]{:S(2)}) async-start(f32[128,64,128]{2,1,0:T(8,128)} %bitcast.35), calls=%async_computation.1 | async-start | bytes 8388608 | tf_op jit(solution)/shard_map/all_to_all | solution.py:438
  63.0 1.1 collective-permute-start.8
  64.3 1.2 slice.66
  66.5 3.4 %shard_map.77.refs_1_.blank = f32[512,4096]{1,0:T(8,128)} custom-call(f32[8,128]{1,0:T(8,128)} %get-tuple-element.15._), custom_call_target="tpu_custom_call" | custom-call | tf_op jit(solution)/shard_map/pallas_call | solution.py:105
  72.8 1.4 constant_dynamic-update-slice_fusion.14.documents
  74.3 7.5 %shard_map.75 = (f32[32,256]{1,0:T(8,128)}, f32[32,4096]{1,0:T(8,128)}) custom-call(f32[32,4096]{1,0:T(8,128)} %copy-done.2, f32[256,4096]{1,0:T(8,128)} %constant_dynamic-update-slice_fusion.14.documents), custom_call_target="tpu_custom_call" | custom-call | tf_op jit(solution)/shard_map/pallas_call | solution.py:140
  84.2 30.5 %all-to-all-done.1 = f32[128,64,128]{2,1,0:T(8,128)} async-done(((f32[128,64,128]{2,1,0:T(8,128)}), f32[128,64,128]{2,1,0:T(8,128)}, u32[]{:S(2)}, u32[]{:S(2)}) %all-to-all-start.1) | async-done | bytes 4194336 | tf_op jit(solution)/shard_map/all_to_all | solution.py:438
  115.5 6.9 %shard_map.78 = (f32[8,256]{1,0:T(8,128)}, f32[8,256]{1,0:T(8,128)}, f32[8,128]{1,0:T(8,128)}) custom-call(f32[32,8,32,128]{3,2,1,0:T(8,128)} %bitcast.13.packed, f32[8,4096]{1,0:T(8,128)} %queries.1, f32[8,4096]{1,0:T(8,128)} %documents.1, s32[1,256]{1,0:T(1,128)} %bitcast.50, s32[256,128]{1,0:T(8,128)} %broadcast_in_dim.157.named, f32[32]{0:T(128)} %copy-done.10, ...), custom_call_target="tpu_custom_call" | custom-call | flops 50331648 | bytes 4194304 | tf_op jit(solution)/shard_map/pallas_call | solution.py:199
  125.4 4.3 %all-to-all-start.2 = ((f32[128,1,314]{2,1,0:T(1,128)}), f32[128,1,314]{2,1,0:T(1,128)S(1)}, u32[]{:S(2)}, u32[]{:S(2)}) async-start(f32[128,1,314]{2,1,0:T(1,128)} %copy.60), calls=%async_computation.2 | async-start | bytes 393216 | tf_op jit(solution)/shard_map/all_to_all | solution.py:438
  129.8 3.0 %collective-permute-start.9 = (f32[8,4096]{1,0:T(8,128)S(1)}, f32[8,4096]{1,0:T(8,128)S(1)}, u32[]{:S(2)}, u32[]{:S(2)}) collective-permute-start(f32[8,4096]{1,0:T(8,128)S(1)} %get-tuple-element.38), channel_id=1, source_target_pairs={{0,2},{1,3},{2,0},{3,1},{4,6},{5,7},{6,4},{7,5},{8,10},{9,11},{10,... | collective-permute-start | bytes 393224 | tf_op jit(solution)/shard_map/ppermute | solution.py:398
  133.6 5.0 %shard_map.79 = f32[8,4096]{1,0:T(8,128)} custom-call(f32[32,8,32,128]{3,2,1,0:T(8,128)} %bitcast.13.packed, f32[8,256]{1,0:T(8,128)} %get-tuple-element.19.scaled, s32[256,128]{1,0:T(8,128)} %broadcast_in_dim.157.named), custom_call_target="tpu_custom_call" | custom-call | flops 50331648 | bytes 4194304 | tf_op jit(solution)/shard_map/pallas_call | solution.py:239
  138.6 2.6 %all-to-all-done.2 = f32[128,1,314]{2,1,0:T(1,128)S(1)} async-done(((f32[128,1,314]{2,1,0:T(1,128)}), f32[128,1,314]{2,1,0:T(1,128)S(1)}, u32[]{:S(2)}, u32[]{:S(2)}) %all-to-all-start.2) | async-done | bytes 160800 | tf_op jit(solution)/shard_map/all_to_all | solution.py:438
  149.6 17.8 %shard_map.80 = (f32[8,4096]{1,0:T(8,128)}, f32[512,4096]{1,0:T(8,128)}) custom-call(s32[1]{0:T(128)} %bitcast.18.count, s32[256]{0:T(256)} %get-tuple-element.28.slot_of, s32[256]{0:T(256)} %get-tuple-element.27.row_of, f32[272,1024]{1,0:T(8,128)} %select_maximum_fusion.weight, ...), custom_call_target="tpu_custom_call", output_to_operand_aliasing={{1}: (8, {})} | custom-call | flops 6845104128 | bytes 25165824 | tf_op jit(solution)/shard_map/pallas_call | solution.py:354
  (140 shorter events, 28.3 us)
Async XLA Ops:
  7.2 28.5 %copy-start = (f32[8,4096]{1,0:T(8,128)S(1)}, f32[8,4096]{1,0:T(8,128)}, u32[]{:S(2)}) copy-start(f32[8,4096]{1,0:T(8,128)} %queries.1) | copy-start | bytes 393220
  7.2 141.7 %all-gather.2.cloned.1.call-start = ((), (), s32[]{:S(2)}) async-start(), calls=%async_computation.3 | async-start | bytes 16908288 | tf_op jit(solution)/shard_map/all_gather | solution.py:454
  7.9 22.1 %collective-permute-start.4 = (f32[8,4096]{1,0:T(8,128)}, f32[8,4096]{1,0:T(8,128)S(1)}, u32[]{:S(2)}, u32[]{:S(2)}) collective-permute-start(f32[8,4096]{1,0:T(8,128)} %documents.1), channel_id=1, source_target_pairs={{96,0},{100,4},{104,8},{108,12},{112,16},{116,20},{120,24},{124,28... | collective-permute-start | bytes 393224 | tf_op jit(solution)/shard_map/ppermute | solution.py:419
  10.4 18.8 %collective-permute-start.3 = (f32[8,4096]{1,0:T(8,128)}, f32[8,4096]{1,0:T(8,128)S(1)}, u32[]{:S(2)}, u32[]{:S(2)}) collective-permute-start(f32[8,4096]{1,0:T(8,128)} %documents.1), channel_id=1, source_target_pairs={{64,0},{68,4},{72,8},{76,12},{80,16},{84,20},{88,24},{92,28},{96,3... | collective-permute-start | bytes 393224 | tf_op jit(solution)/shard_map/ppermute | solution.py:419
  13.7 14.8 %collective-permute-start.2 = (f32[8,4096]{1,0:T(8,128)}, f32[8,4096]{1,0:T(8,128)S(1)}, u32[]{:S(2)}, u32[]{:S(2)}) collective-permute-start(f32[8,4096]{1,0:T(8,128)} %documents.1), channel_id=1, source_target_pairs={{32,0},{36,4},{40,8},{44,12},{48,16},{52,20},{56,24},{60,28},{64,3... | collective-permute-start | bytes 393224 | tf_op jit(solution)/shard_map/ppermute | solution.py:419
  14.5 21.2 %collective-permute-start = (f32[8,4096]{1,0:T(8,128)}, f32[8,4096]{1,0:T(8,128)S(1)}, u32[]{:S(2)}, u32[]{:S(2)}) collective-permute-start(f32[8,4096]{1,0:T(8,128)} %queries.1), channel_id=1, source_target_pairs={{0,2},{1,3},{2,0},{3,1},{4,6},{5,7},{6,4},{7,5},{8,10},{9,11},{10,... | collective-permute-start | bytes 393224 | tf_op jit(solution)/shard_map/ppermute | solution.py:398
  19.3 23.1 %all-to-all-start = ((s32[128,1,128]{2,1,0:T(1,128)}), s32[128,1,128]{2,1,0:T(1,128)S(1)}, u32[]{:S(2)}, u32[]{:S(2)}) async-start(s32[128,1,128]{2,1,0:T(1,128)} %bitcast.8), calls=%async_computation | async-start | bytes 131072 | tf_op jit(solution)/shard_map/all_to_all | solution.py:438
  30.7 11.7 %copy-start.6 = (f32[32,4096]{1,0:T(8,128)}, f32[32,4096]{1,0:T(8,128)S(1)}, u32[]{:S(2)}) copy-start(f32[32,4096]{1,0:T(8,128)S(1)} %get-tuple-element.50.refs_0_) | copy-start | bytes 1572868
  30.7 31.3 %collective-permute-start.7 = (f32[32,4096]{1,0:T(8,128)S(1)}, f32[32,4096]{1,0:T(8,128)S(1)}, u32[]{:S(2)}, u32[]{:S(2)}) collective-permute-start(f32[32,4096]{1,0:T(8,128)S(1)} %get-tuple-element.50.refs_0_), channel_id=1, source_target_pairs={{24,0},{28,4},{0,8},{4,12},{8,16},{12,20},{16,24},{20,28},{56,32},... | collective-permute-start | bytes 1572872 | tf_op jit(solution)/shard_map/ppermute | solution.py:419
  32.1 28.9 %collective-permute-start.6 = (f32[32,4096]{1,0:T(8,128)S(1)}, f32[32,4096]{1,0:T(8,128)S(1)}, u32[]{:S(2)}, u32[]{:S(2)}) collective-permute-start(f32[32,4096]{1,0:T(8,128)S(1)} %get-tuple-element.50.refs_0_), channel_id=1, source_target_pairs={{16,0},{20,4},{24,8},{28,12},{0,16},{4,20},{8,24},{12,28},{48,32},... | collective-permute-start | bytes 1572872 | tf_op jit(solution)/shard_map/ppermute | solution.py:419
  34.5 25.3 %collective-permute-start.5 = (f32[32,4096]{1,0:T(8,128)S(1)}, f32[32,4096]{1,0:T(8,128)S(1)}, u32[]{:S(2)}, u32[]{:S(2)}) collective-permute-start(f32[32,4096]{1,0:T(8,128)S(1)} %get-tuple-element.50.refs_0_), channel_id=1, source_target_pairs={{8,0},{12,4},{16,8},{20,12},{24,16},{28,20},{0,24},{4,28},{40,32},... | collective-permute-start | bytes 1572872 | tf_op jit(solution)/shard_map/ppermute | solution.py:419
  35.7 6.7 %collective-permute-start.1 = (f32[16,4096]{1,0:T(8,128)S(1)}, f32[16,4096]{1,0:T(8,128)S(1)}, u32[]{:S(2)}, u32[]{:S(2)}) collective-permute-start(f32[16,4096]{1,0:T(8,128)S(1)} %pad_maximum_fusion), channel_id=1, source_target_pairs={{0,1},{1,0},{2,3},{3,2},{4,5},{5,4},{6,7},{7,6},{8,9},{9,8},{10,11... | collective-permute-start | bytes 786440 | tf_op jit(solution)/shard_map/ppermute | solution.py:398
  51.1 63.6 %all-to-all-start.1 = ((f32[128,64,128]{2,1,0:T(8,128)}), f32[128,64,128]{2,1,0:T(8,128)}, u32[]{:S(2)}, u32[]{:S(2)}) async-start(f32[128,64,128]{2,1,0:T(8,128)} %bitcast.35), calls=%async_computation.1 | async-start | bytes 8388608 | tf_op jit(solution)/shard_map/all_to_all | solution.py:438
  60.9 5.2 %copy-start.5 = (s32[128,1,128]{2,1,0:T(1,128)S(1)}, s32[128,1,128]{2,1,0:T(1,128)}, u32[]{:S(2)}) copy-start(s32[128,1,128]{2,1,0:T(1,128)} %copy-done.4) | copy-start | bytes 196612
  63.0 9.9 %collective-permute-start.8 = (f32[128,4096]{1,0:T(8,128)}, f32[128,4096]{1,0:T(8,128)S(1)}, u32[]{:S(2)}, u32[]{:S(2)}) collective-permute-start(f32[128,4096]{1,0:T(8,128)} %get-tuple-element.41), channel_id=1, source_target_pairs={{4,0},{0,4},{12,8},{8,12},{20,16},{16,20},{28,24},{24,28},{36,32},... | collective-permute-start | bytes 6291464 | tf_op jit(solution)/shard_map/ppermute | solution.py:419
  64.3 50.4 %copy-start.9 = (s32[256]{0:T(256)}, s32[256]{0:T(256)S(1)}, u32[]{:S(2)}) copy-start(s32[256]{0:T(256)S(1)} %broadcast_add_fusion) | copy-start | bytes 3076
  82.7 32.8 %copy-start.10 = (f32[32]{0:T(128)}, f32[32]{0:T(128)S(1)}, u32[]{:S(2)}) copy-start(f32[32]{0:T(128)S(1)} %reduce_sum.108.refs_0_) | copy-start | bytes 388
  115.5 14.2 %copy-start.8 = (f32[32,4096]{1,0:T(8,128)S(1)}, f32[32,4096]{1,0:T(8,128)}, u32[]{:S(2)}) copy-start(f32[32,4096]{1,0:T(8,128)} %get-tuple-element.18) | copy-start | bytes 1572868
  125.4 15.8 %all-to-all-start.2 = ((f32[128,1,314]{2,1,0:T(1,128)}), f32[128,1,314]{2,1,0:T(1,128)S(1)}, u32[]{:S(2)}, u32[]{:S(2)}) async-start(f32[128,1,314]{2,1,0:T(1,128)} %copy.60), calls=%async_computation.2 | async-start | bytes 393216 | tf_op jit(solution)/shard_map/all_to_all | solution.py:438
  129.8 16.6 %collective-permute-start.9 = (f32[8,4096]{1,0:T(8,128)S(1)}, f32[8,4096]{1,0:T(8,128)S(1)}, u32[]{:S(2)}, u32[]{:S(2)}) collective-permute-start(f32[8,4096]{1,0:T(8,128)S(1)} %get-tuple-element.38), channel_id=1, source_target_pairs={{0,2},{1,3},{2,0},{3,1},{4,6},{5,7},{6,4},{7,5},{8,10},{9,11},{10,... | collective-permute-start | bytes 393224 | tf_op jit(solution)/shard_map/ppermute | solution.py:398
  132.7 13.6 %collective-permute-start.11 = (f32[8,4096]{1,0:T(8,128)S(1)}, f32[8,4096]{1,0:T(8,128)S(1)}, u32[]{:S(2)}, u32[]{:S(2)}) collective-permute-start(f32[8,4096]{1,0:T(8,128)S(1)} %get-tuple-element.39), channel_id=1, source_target_pairs={{0,3},{1,2},{2,1},{3,0},{4,7},{5,6},{6,5},{7,4},{8,11},{9,10},{10,... | collective-permute-start | bytes 393224 | tf_op jit(solution)/shard_map/ppermute | solution.py:398
  133.6 12.8 %collective-permute-start.10 = (f32[8,4096]{1,0:T(8,128)S(1)}, f32[8,4096]{1,0:T(8,128)S(1)}, u32[]{:S(2)}, u32[]{:S(2)}) collective-permute-start(f32[8,4096]{1,0:T(8,128)S(1)} %get-tuple-element.40), channel_id=1, source_target_pairs={{0,1},{1,0},{2,3},{3,2},{4,5},{5,4},{6,7},{7,6},{8,9},{9,8},{10,11... | collective-permute-start | bytes 393224 | tf_op jit(solution)/shard_map/ppermute | solution.py:398
  143.4 3.0 %copy-start.1 = (f32[8,4096]{1,0:T(8,128)S(1)}, f32[8,4096]{1,0:T(8,128)}, u32[]{:S(2)}) copy-start(f32[8,4096]{1,0:T(8,128)} %queries.1) | copy-start | bytes 393220
  143.4 3.0 %copy-start.3 = (f32[8,4096]{1,0:T(8,128)S(1)}, f32[8,4096]{1,0:T(8,128)}, u32[]{:S(2)}) copy-start(f32[8,4096]{1,0:T(8,128)} %documents.1) | copy-start | bytes 393220
  (3 other events, 4.6 us)
Sparse Core Ops, SparseCore 0:
  11.1 137.7 all-gather.1

commit v2 on v1

--- a/solution.py
+++ b/solution.py
@@ -36,7 +36,7 @@
     def fetch(code, tile, slot):
         row = lax.div(code, own)
         return pltpu.make_async_copy(
-            pool.at[lax.div(row, 8), :, lax.rem(row, 8)], held.at[tile, slot], landed
+            pool.at[lax.div(row, 8), :, lax.rem(row, 8)], held.at[tile, slot], landed.at[lax.div(tile, part)]
         )
 
     def start(tile, count):
@@ -50,16 +50,18 @@
             count = count + (code >= 0).astype(jnp.int32)
         return count
 
-    def wait(j, carry):
-        fetch(0, 0, 0).wait()
-        return carry
-
     def send(i):
         rows = pl.ds(i * part, part)
         return pltpu.make_async_copy(held.at[rows], packed.at[rows], sent.at[i])
 
-    lax.fori_loop(0, lax.fori_loop(0, held.shape[0], start, 0), wait, 0)
+    counts = [lax.fori_loop(i * part, (i + 1) * part, start, 0) for i in range(pieces)]
     for i in range(pieces):
+
+        def wait(j, carry, i=i):
+            fetch(0, i * part, 0).wait()
+            return carry
+
+        lax.fori_loop(0, counts[i], wait, 0)
         send(i).start()
     done[...] = jnp.zeros_like(done)
     for i in range(pieces):
@@ -78,7 +80,7 @@
         out_specs=[anywhere, pl.BlockSpec(memory_space=pltpu.VMEM)],
         scratch_shapes=[
             pltpu.VMEM(shape, jnp.float32),
-            pltpu.SemaphoreType.DMA,
+            pltpu.SemaphoreType.DMA((4,)),
             pltpu.SemaphoreType.DMA((4,)),
         ],
         out_shape=[jax.ShapeDtypeStruct(shape, jnp.float32), jax.ShapeDtypeStruct((8, lanes), jnp.float32)],

time: 175 us -> 174 us (level)
  transfers between devices with their start and end apart: 16 -> 16, of which waited for: 4 -> 3; matrix products, arithmetic and copies ran while one was open for 16% -> 16% of each run, Pallas kernels for 17% -> 17%
where the time goes in v2:
time: 174 us
  Pallas kernels  48.2 us (28%)
  starting transfers between devices  40.7 us (23%)
  waiting for transfers between devices  39.1 us (22%)
  local copies, waits for them, and re-layouts  20.4 us (12%)
  between operations  17.1 us (10%)
  other arithmetic  8 us (5%)
    all_to_all x3, waiting for transfers between devices, exchange(): lax.all_to_all(values, everyone, split_axis=0, concat_axis=0, tiled=True)  33 us
    all_to_all x3, starting transfers between devices, exchange(): lax.all_to_all(values, everyone, split_axis=0, concat_axis=0, tiled=True)  20 us
    pallas_call x1, Pallas kernels, finish(): pl.pallas_call(finish_kernel, in_specs=[smem, smem, smem, anywhere, anywh...  17.7 us
    ppermute x7, starting transfers between devices, ahead(): blocks.append(lax.ppermute(values, 'dp', pairs))  12.7 us
    ppermute x5, starting transfers between devices, swap(): return lax.ppermute(values, 'pool', [(i, i ^ bits) for i in range(4)])  8.04 us
    pallas_call x1, Pallas kernels, pick(): pl.pallas_call(functools.partial(pick_kernel, own), in_specs=[pl.BlockSpe...  7.66 us
    unnamed x30, local copies, waits for them, and re-layouts  7.66 us
    pallas_call x1, Pallas kernels, beside(): pl.pallas_call(beside_kernel, in_specs=[vmem, vmem], out_specs=[vmem, vme...  7.55 us
  transfers between devices with their start and end apart: 16, of which 3 were waited for; matrix products, arithmetic and copies ran while one was open for 16% of the time, Pallas kernels for 17%

profile of v2, /device:TPU:1, one launch (start us, length us, event | category | flops | bytes accessed | tf_op | source)
XLA Modules:
  0.0 174.4 jit_solution(11798805148346961512)
XLA Ops:
  7.9 2.5 %collective-permute-start.4 = (f32[8,4096]{1,0:T(8,128)}, f32[8,4096]{1,0:T(8,128)S(1)}, u32[]{:S(2)}, u32[]{:S(2)}) collective-permute-start(f32[8,4096]{1,0:T(8,128)} %documents.1), channel_id=1, source_target_pairs={{96,0},{100,4},{104,8},{108,12},{112,16},{116,20},{120,24},{124,28... | collective-permute-start | bytes 393224 | tf_op jit(solution)/shard_map/ppermute | solution.py:421
  10.4 3.3 %collective-permute-start.3 = (f32[8,4096]{1,0:T(8,128)}, f32[8,4096]{1,0:T(8,128)S(1)}, u32[]{:S(2)}, u32[]{:S(2)}) collective-permute-start(f32[8,4096]{1,0:T(8,128)} %documents.1), channel_id=1, source_target_pairs={{64,0},{68,4},{72,8},{76,12},{80,16},{84,20},{88,24},{92,28},{96,3... | collective-permute-start | bytes 393224 | tf_op jit(solution)/shard_map/ppermute | solution.py:421
  14.5 2.9 %collective-permute-start = (f32[8,4096]{1,0:T(8,128)}, f32[8,4096]{1,0:T(8,128)S(1)}, u32[]{:S(2)}, u32[]{:S(2)}) collective-permute-start(f32[8,4096]{1,0:T(8,128)} %queries.1), channel_id=1, source_target_pairs={{0,2},{1,3},{2,0},{3,1},{4,6},{5,7},{6,4},{7,5},{8,10},{9,11},{10,... | collective-permute-start | bytes 393224 | tf_op jit(solution)/shard_map/ppermute | solution.py:400
  19.3 6.6 %all-to-all-start = ((s32[128,1,128]{2,1,0:T(1,128)}), s32[128,1,128]{2,1,0:T(1,128)S(1)}, u32[]{:S(2)}, u32[]{:S(2)}) async-start(s32[128,1,128]{2,1,0:T(1,128)} %bitcast.8), calls=%async_computation | async-start | bytes 131072 | tf_op jit(solution)/shard_map/all_to_all | solution.py:440
  26.0 1.6 constant_dynamic-update-slice_fusion.13
  30.7 1.4 collective-permute-start.7
  32.1 2.4 %collective-permute-start.6 = (f32[32,4096]{1,0:T(8,128)S(1)}, f32[32,4096]{1,0:T(8,128)S(1)}, u32[]{:S(2)}, u32[]{:S(2)}) collective-permute-start(f32[32,4096]{1,0:T(8,128)S(1)} %get-tuple-element.50.refs_0_), channel_id=1, source_target_pairs={{16,0},{20,4},{24,8},{28,12},{0,16},{4,20},{8,24},{12,28},{48,32},... | collective-permute-start | bytes 1572872 | tf_op jit(solution)/shard_map/ppermute | solution.py:421
  34.5 1.2 collective-permute-start.5
  35.7 1.3 collective-permute-start.1
  36.9 5.4 %collective-permute-done.1 = f32[16,4096]{1,0:T(8,128)S(1)} collective-permute-done((f32[16,4096]{1,0:T(8,128)S(1)}, f32[16,4096]{1,0:T(8,128)S(1)}, u32[]{:S(2)}, u32[]{:S(2)}) %collective-permute-start.1) | collective-permute-done | bytes 262176 | tf_op jit(solution)/shard_map/ppermute | solution.py:400
  43.2 7.7 %shard_map.76 = (f32[32,8,32,128]{3,2,1,0:T(8,128)}, f32[8,128]{1,0:T(8,128)}) custom-call(s32[128,128]{1,0:T(8,128)} %bitcast.37, f32[64,32,8,128]{3,2,1,0:T(8,128)} %bitcast.36, f32[32,4096]{1,0:T(8,128)} %copy-done.6, f32[32,4096]{1,0:T(8,128)} %copy-done.2), custom_call_target="tpu_custom_call" | custom-call | bytes 8388608 | tf_op jit(solution)/shard_map/pallas_call | solution.py:77
  50.9 9.4 %all-to-all-start.1 = ((f32[128,64,128]{2,1,0:T(8,128)}), f32[128,64,128]{2,1,0:T(8,128)}, u32[]{:S(2)}, u32[]{:S(2)}) async-start(f32[128,64,128]{2,1,0:T(8,128)} %bitcast.35), calls=%async_computation.1 | async-start | bytes 8388608 | tf_op jit(solution)/shard_map/all_to_all | solution.py:440
  63.4 1.1 collective-permute-start.8
  64.7 1.2 slice.66
  67.0 3.4 %shard_map.77.refs_1_.blank = f32[512,4096]{1,0:T(8,128)} custom-call(f32[8,128]{1,0:T(8,128)} %get-tuple-element.15._), custom_call_target="tpu_custom_call" | custom-call | tf_op jit(solution)/shard_map/pallas_call | solution.py:107
  73.3 1.4 constant_dynamic-update-slice_fusion.14.documents
  74.7 7.5 %shard_map.75 = (f32[32,256]{1,0:T(8,128)}, f32[32,4096]{1,0:T(8,128)}) custom-call(f32[32,4096]{1,0:T(8,128)} %copy-done.2, f32[256,4096]{1,0:T(8,128)} %constant_dynamic-update-slice_fusion.14.documents), custom_call_target="tpu_custom_call" | custom-call | tf_op jit(solution)/shard_map/pallas_call | solution.py:142
  84.7 30.3 %all-to-all-done.1 = f32[128,64,128]{2,1,0:T(8,128)} async-done(((f32[128,64,128]{2,1,0:T(8,128)}), f32[128,64,128]{2,1,0:T(8,128)}, u32[]{:S(2)}, u32[]{:S(2)}) %all-to-all-start.1) | async-done | bytes 4194336 | tf_op jit(solution)/shard_map/all_to_all | solution.py:440
  115.8 6.9 %shard_map.78 = (f32[8,256]{1,0:T(8,128)}, f32[8,256]{1,0:T(8,128)}, f32[8,128]{1,0:T(8,128)}) custom-call(f32[32,8,32,128]{3,2,1,0:T(8,128)} %bitcast.13.packed, f32[8,4096]{1,0:T(8,128)} %queries.1, f32[8,4096]{1,0:T(8,128)} %documents.1, s32[1,256]{1,0:T(1,128)} %bitcast.50, s32[256,128]{1,0:T(8,128)} %broadcast_in_dim.157.named, f32[32]{0:T(128)} %copy-done.10, ...), custom_call_target="tpu_custom_call" | custom-call | flops 50331648 | bytes 4194304 | tf_op jit(solution)/shard_map/pallas_call | solution.py:201
  125.8 3.9 %all-to-all-start.2 = ((f32[128,1,314]{2,1,0:T(1,128)}), f32[128,1,314]{2,1,0:T(1,128)S(1)}, u32[]{:S(2)}, u32[]{:S(2)}) async-start(f32[128,1,314]{2,1,0:T(1,128)} %copy.60), calls=%async_computation.2 | async-start | bytes 393216 | tf_op jit(solution)/shard_map/all_to_all | solution.py:440
  129.8 3.0 %collective-permute-start.9 = (f32[8,4096]{1,0:T(8,128)S(1)}, f32[8,4096]{1,0:T(8,128)S(1)}, u32[]{:S(2)}, u32[]{:S(2)}) collective-permute-start(f32[8,4096]{1,0:T(8,128)S(1)} %get-tuple-element.38), channel_id=1, source_target_pairs={{0,2},{1,3},{2,0},{3,1},{4,6},{5,7},{6,4},{7,5},{8,10},{9,11},{10,... | collective-permute-start | bytes 393224 | tf_op jit(solution)/shard_map/ppermute | solution.py:400
  133.6 4.9 %shard_map.79 = f32[8,4096]{1,0:T(8,128)} custom-call(f32[32,8,32,128]{3,2,1,0:T(8,128)} %bitcast.13.packed, f32[8,256]{1,0:T(8,128)} %get-tuple-element.19.scaled, s32[256,128]{1,0:T(8,128)} %broadcast_in_dim.157.named), custom_call_target="tpu_custom_call" | custom-call | flops 50331648 | bytes 4194304 | tf_op jit(solution)/shard_map/pallas_call | solution.py:241
  138.5 2.7 %all-to-all-done.2 = f32[128,1,314]{2,1,0:T(1,128)S(1)} async-done(((f32[128,1,314]{2,1,0:T(1,128)}), f32[128,1,314]{2,1,0:T(1,128)S(1)}, u32[]{:S(2)}, u32[]{:S(2)}) %all-to-all-start.2) | async-done | bytes 160800 | tf_op jit(solution)/shard_map/all_to_all | solution.py:440
  148.7 17.7 %shard_map.80 = (f32[8,4096]{1,0:T(8,128)}, f32[512,4096]{1,0:T(8,128)}) custom-call(s32[1]{0:T(128)} %bitcast.18.count, s32[256]{0:T(256)} %get-tuple-element.28.slot_of, s32[256]{0:T(256)} %get-tuple-element.27.row_of, f32[272,1024]{1,0:T(8,128)} %select_maximum_fusion.weight, ...), custom_call_target="tpu_custom_call", output_to_operand_aliasing={{1}: (8, {})} | custom-call | flops 6845104128 | bytes 25165824 | tf_op jit(solution)/shard_map/pallas_call | solution.py:356
  (140 shorter events, 27.4 us)
Async XLA Ops:
  7.2 28.5 %copy-start = (f32[8,4096]{1,0:T(8,128)S(1)}, f32[8,4096]{1,0:T(8,128)}, u32[]{:S(2)}) copy-start(f32[8,4096]{1,0:T(8,128)} %queries.1) | copy-start | bytes 393220
  7.2 140.9 %all-gather.2.cloned.1.call-start = ((), (), s32[]{:S(2)}) async-start(), calls=%async_computation.3 | async-start | bytes 16908288 | tf_op jit(solution)/shard_map/all_gather | solution.py:456
  7.9 22.1 %collective-permute-start.4 = (f32[8,4096]{1,0:T(8,128)}, f32[8,4096]{1,0:T(8,128)S(1)}, u32[]{:S(2)}, u32[]{:S(2)}) collective-permute-start(f32[8,4096]{1,0:T(8,128)} %documents.1), channel_id=1, source_target_pairs={{96,0},{100,4},{104,8},{108,12},{112,16},{116,20},{120,24},{124,28... | collective-permute-start | bytes 393224 | tf_op jit(solution)/shard_map/ppermute | solution.py:421
  10.4 18.8 %collective-permute-start.3 = (f32[8,4096]{1,0:T(8,128)}, f32[8,4096]{1,0:T(8,128)S(1)}, u32[]{:S(2)}, u32[]{:S(2)}) collective-permute-start(f32[8,4096]{1,0:T(8,128)} %documents.1), channel_id=1, source_target_pairs={{64,0},{68,4},{72,8},{76,12},{80,16},{84,20},{88,24},{92,28},{96,3... | collective-permute-start | bytes 393224 | tf_op jit(solution)/shard_map/ppermute | solution.py:421
  13.7 14.8 %collective-permute-start.2 = (f32[8,4096]{1,0:T(8,128)}, f32[8,4096]{1,0:T(8,128)S(1)}, u32[]{:S(2)}, u32[]{:S(2)}) collective-permute-start(f32[8,4096]{1,0:T(8,128)} %documents.1), channel_id=1, source_target_pairs={{32,0},{36,4},{40,8},{44,12},{48,16},{52,20},{56,24},{60,28},{64,3... | collective-permute-start | bytes 393224 | tf_op jit(solution)/shard_map/ppermute | solution.py:421
  14.5 21.2 %collective-permute-start = (f32[8,4096]{1,0:T(8,128)}, f32[8,4096]{1,0:T(8,128)S(1)}, u32[]{:S(2)}, u32[]{:S(2)}) collective-permute-start(f32[8,4096]{1,0:T(8,128)} %queries.1), channel_id=1, source_target_pairs={{0,2},{1,3},{2,0},{3,1},{4,6},{5,7},{6,4},{7,5},{8,10},{9,11},{10,... | collective-permute-start | bytes 393224 | tf_op jit(solution)/shard_map/ppermute | solution.py:400
  19.3 23.1 %all-to-all-start = ((s32[128,1,128]{2,1,0:T(1,128)}), s32[128,1,128]{2,1,0:T(1,128)S(1)}, u32[]{:S(2)}, u32[]{:S(2)}) async-start(s32[128,1,128]{2,1,0:T(1,128)} %bitcast.8), calls=%async_computation | async-start | bytes 131072 | tf_op jit(solution)/shard_map/all_to_all | solution.py:440
  30.7 11.7 %copy-start.6 = (f32[32,4096]{1,0:T(8,128)}, f32[32,4096]{1,0:T(8,128)S(1)}, u32[]{:S(2)}) copy-start(f32[32,4096]{1,0:T(8,128)S(1)} %get-tuple-element.50.refs_0_) | copy-start | bytes 1572868
  30.7 31.8 %collective-permute-start.7 = (f32[32,4096]{1,0:T(8,128)S(1)}, f32[32,4096]{1,0:T(8,128)S(1)}, u32[]{:S(2)}, u32[]{:S(2)}) collective-permute-start(f32[32,4096]{1,0:T(8,128)S(1)} %get-tuple-element.50.refs_0_), channel_id=1, source_target_pairs={{24,0},{28,4},{0,8},{4,12},{8,16},{12,20},{16,24},{20,28},{56,32},... | collective-permute-start | bytes 1572872 | tf_op jit(solution)/shard_map/ppermute | solution.py:421
  32.1 29.3 %collective-permute-start.6 = (f32[32,4096]{1,0:T(8,128)S(1)}, f32[32,4096]{1,0:T(8,128)S(1)}, u32[]{:S(2)}, u32[]{:S(2)}) collective-permute-start(f32[32,4096]{1,0:T(8,128)S(1)} %get-tuple-element.50.refs_0_), channel_id=1, source_target_pairs={{16,0},{20,4},{24,8},{28,12},{0,16},{4,20},{8,24},{12,28},{48,32},... | collective-permute-start | bytes 1572872 | tf_op jit(solution)/shard_map/ppermute | solution.py:421
  34.5 25.8 %collective-permute-start.5 = (f32[32,4096]{1,0:T(8,128)S(1)}, f32[32,4096]{1,0:T(8,128)S(1)}, u32[]{:S(2)}, u32[]{:S(2)}) collective-permute-start(f32[32,4096]{1,0:T(8,128)S(1)} %get-tuple-element.50.refs_0_), channel_id=1, source_target_pairs={{8,0},{12,4},{16,8},{20,12},{24,16},{28,20},{0,24},{4,28},{40,32},... | collective-permute-start | bytes 1572872 | tf_op jit(solution)/shard_map/ppermute | solution.py:421
  35.7 6.7 %collective-permute-start.1 = (f32[16,4096]{1,0:T(8,128)S(1)}, f32[16,4096]{1,0:T(8,128)S(1)}, u32[]{:S(2)}, u32[]{:S(2)}) collective-permute-start(f32[16,4096]{1,0:T(8,128)S(1)} %pad_maximum_fusion), channel_id=1, source_target_pairs={{0,1},{1,0},{2,3},{3,2},{4,5},{5,4},{6,7},{7,6},{8,9},{9,8},{10,11... | collective-permute-start | bytes 786440 | tf_op jit(solution)/shard_map/ppermute | solution.py:400
  50.9 64.2 %all-to-all-start.1 = ((f32[128,64,128]{2,1,0:T(8,128)}), f32[128,64,128]{2,1,0:T(8,128)}, u32[]{:S(2)}, u32[]{:S(2)}) async-start(f32[128,64,128]{2,1,0:T(8,128)} %bitcast.35), calls=%async_computation.1 | async-start | bytes 8388608 | tf_op jit(solution)/shard_map/all_to_all | solution.py:440
  61.4 5.2 %copy-start.5 = (s32[128,1,128]{2,1,0:T(1,128)S(1)}, s32[128,1,128]{2,1,0:T(1,128)}, u32[]{:S(2)}) copy-start(s32[128,1,128]{2,1,0:T(1,128)} %copy-done.4) | copy-start | bytes 196612
  63.4 9.9 %collective-permute-start.8 = (f32[128,4096]{1,0:T(8,128)}, f32[128,4096]{1,0:T(8,128)S(1)}, u32[]{:S(2)}, u32[]{:S(2)}) collective-permute-start(f32[128,4096]{1,0:T(8,128)} %get-tuple-element.41), channel_id=1, source_target_pairs={{4,0},{0,4},{12,8},{8,12},{20,16},{16,20},{28,24},{24,28},{36,32},... | collective-permute-start | bytes 6291464 | tf_op jit(solution)/shard_map/ppermute | solution.py:421
  64.7 50.3 %copy-start.9 = (s32[256]{0:T(256)}, s32[256]{0:T(256)S(1)}, u32[]{:S(2)}) copy-start(s32[256]{0:T(256)S(1)} %broadcast_add_fusion) | copy-start | bytes 3076
  83.2 32.6 %copy-start.10 = (f32[32]{0:T(128)}, f32[32]{0:T(128)S(1)}, u32[]{:S(2)}) copy-start(f32[32]{0:T(128)S(1)} %reduce_sum.108.refs_0_) | copy-start | bytes 388
  115.8 13.9 %copy-start.8 = (f32[32,4096]{1,0:T(8,128)S(1)}, f32[32,4096]{1,0:T(8,128)}, u32[]{:S(2)}) copy-start(f32[32,4096]{1,0:T(8,128)} %get-tuple-element.18) | copy-start | bytes 1572868
  125.8 15.4 %all-to-all-start.2 = ((f32[128,1,314]{2,1,0:T(1,128)}), f32[128,1,314]{2,1,0:T(1,128)S(1)}, u32[]{:S(2)}, u32[]{:S(2)}) async-start(f32[128,1,314]{2,1,0:T(1,128)} %copy.60), calls=%async_computation.2 | async-start | bytes 393216 | tf_op jit(solution)/shard_map/all_to_all | solution.py:440
  129.8 16.6 %collective-permute-start.9 = (f32[8,4096]{1,0:T(8,128)S(1)}, f32[8,4096]{1,0:T(8,128)S(1)}, u32[]{:S(2)}, u32[]{:S(2)}) collective-permute-start(f32[8,4096]{1,0:T(8,128)S(1)} %get-tuple-element.38), channel_id=1, source_target_pairs={{0,2},{1,3},{2,0},{3,1},{4,6},{5,7},{6,4},{7,5},{8,10},{9,11},{10,... | collective-permute-start | bytes 393224 | tf_op jit(solution)/shard_map/ppermute | solution.py:400
  132.7 13.7 %collective-permute-start.11 = (f32[8,4096]{1,0:T(8,128)S(1)}, f32[8,4096]{1,0:T(8,128)S(1)}, u32[]{:S(2)}, u32[]{:S(2)}) collective-permute-start(f32[8,4096]{1,0:T(8,128)S(1)} %get-tuple-element.39), channel_id=1, source_target_pairs={{0,3},{1,2},{2,1},{3,0},{4,7},{5,6},{6,5},{7,4},{8,11},{9,10},{10,... | collective-permute-start | bytes 393224 | tf_op jit(solution)/shard_map/ppermute | solution.py:400
  133.6 12.8 %collective-permute-start.10 = (f32[8,4096]{1,0:T(8,128)S(1)}, f32[8,4096]{1,0:T(8,128)S(1)}, u32[]{:S(2)}, u32[]{:S(2)}) collective-permute-start(f32[8,4096]{1,0:T(8,128)S(1)} %get-tuple-element.40), channel_id=1, source_target_pairs={{0,1},{1,0},{2,3},{3,2},{4,5},{5,4},{6,7},{7,6},{8,9},{9,8},{10,11... | collective-permute-start | bytes 393224 | tf_op jit(solution)/shard_map/ppermute | solution.py:400
  143.4 3.0 %copy-start.1 = (f32[8,4096]{1,0:T(8,128)S(1)}, f32[8,4096]{1,0:T(8,128)}, u32[]{:S(2)}) copy-start(f32[8,4096]{1,0:T(8,128)} %queries.1) | copy-start | bytes 393220
  143.4 3.0 %copy-start.3 = (f32[8,4096]{1,0:T(8,128)S(1)}, f32[8,4096]{1,0:T(8,128)}, u32[]{:S(2)}) copy-start(f32[8,4096]{1,0:T(8,128)} %documents.1) | copy-start | bytes 393220
  (3 other events, 4.6 us)
Sparse Core Ops, SparseCore 0:
  11.1 130.6 all-gather.1
